TPU v7x, 32 devices: a whole 2x2x4 slice. The times are simulated.
32 devices in a mesh: gx: 8 (over z, y), gy: 2 (over x), gz: 2 (over core).
Axes of the slice: x: 2, y: 2, z: 4, core: 2. Of those that a mesh axis runs over, the one named last changes fastest.
Arguments:
- pops: float32 [19, 32, 64, 256], P(None, 'gz', 'gx', 'gy'), as said below
- solid: int32 [32, 64, 256], P('gz', 'gx', 'gy'), may hold values 0 or 1
- surf_cell: int32 [2, 8, 2, 512], P('gz', 'gx', 'gy'), may hold values from 0 to 16383
- surf_panel: int32 [2, 8, 2, 512], P('gz', 'gx', 'gy'), may hold values from -1 to 39, as said below
- surf_area: float32 [2, 8, 2, 512], P('gz', 'gx', 'gy'), may hold values from 0.1 to 1
- mode_shape: float32 [2, 8, 2, 12, 512], P('gz', 'gx', 'gy'), may hold values from -5 to 5
- mode_of_panel: int32 [40], replicated, may hold values from 0 to 11
- compliance: float32 [12], replicated, may hold values from 0.3 to 3
Outputs:
- read: float32 [19, 32, 64, 256], P(None, 'gz', 'gx', 'gy')
- panel_force: float32 [40], replicated
- mode_amplitude: float32 [12], replicated
Inputs may be any that keep to these rules, and one draw needn't show every extreme that they name: pops is positive, with densities near 1 and flow speeds below 0.25. `surf_panel`: -1 marks an empty slot; on each device the live slots come first, at least 64 of them; some device has all 512 slots live; one panel's surfels lie on at most about 40 consecutive bricks in the linear order (vertical, streamwise, crosswise) of the devices, counted periodically so that the last brick is followed by the first.
All inputs are finite; a program needn't handle non-finite values. No bound on the sum of `solid` on one device may be relied on, other than what follows from the above.
Results may differ from a plain program's by a relative error of at most 0.00011.
Values sent between devices are 32-bit elements; how exact they have to be, the bound alone decides.
A program may use at most 64 MiB of HBM per device.

v0:
```python
import functools

import jax
import jax.numpy as jnp
from jax import lax
from jax.experimental import pallas as pl
from jax.experimental.pallas import tpu as pltpu
from jax.sharding import PartitionSpec as P

PANELS = 40
MODES = 12
VELOCITY = (
    (0, 0, 0),
    (1, 0, 0),
    (-1, 0, 0),
    (0, 1, 0),
    (0, -1, 0),
    (0, 0, 1),
    (0, 0, -1),
    (1, 1, 0),
    (-1, -1, 0),
    (1, -1, 0),
    (-1, 1, 0),
    (1, 0, 1),
    (-1, 0, -1),
    (1, 0, -1),
    (-1, 0, 1),
    (0, 1, 1),
    (0, -1, -1),
    (0, 1, -1),
    (0, -1, 1),
)
WEIGHTS = (1.0 / 3.0,) + (1.0 / 18.0,) * 6 + (1.0 / 36.0,) * 12
OMEGA = 1.0 / 0.6
WALL_SCALE = 0.02
COEF = tuple(6.0 * w * v[0] for w, v in zip(WEIGHTS, VELOCITY))
SIGNS = (1, -1)


def moving(axis, sign):
    return tuple(i for i in range(19) if VELOCITY[i][axis] == sign)


X_GROUP = tuple(moving(0, s) for s in SIGNS)
Y_GROUP = tuple(moving(1, s) for s in SIGNS)
Z_GROUP = tuple(moving(2, s) for s in SIGNS)
ORDER = Z_GROUP[0] + Z_GROUP[1] + tuple(i for i in range(19) if VELOCITY[i][2] == 0)
PLACE = tuple(ORDER.index(i) for i in range(19))
AXES = ("gx", "gy", "gz")
STAGES = (("gx",), ("gy", "gz"))
MESH = pl.DeviceIdType.MESH
N_LOADS = 4
F32 = jnp.float32
BF16 = jnp.bfloat16


def halves(x):
    high = x.astype(BF16)
    return high, (x - high.astype(F32)).astype(BF16)


def dot(a, b):
    return jnp.dot(a, b, preferred_element_type=F32)


def dot_nt(a, b):
    return lax.dot_general(a, b, (((1,), (1,)), ((), ())), preferred_element_type=F32)


def shift_of(velocity):
    return (velocity[0], velocity[1], velocity[2])


def offsets_of(sizes):
    found = []
    for i in range(1, 19):
        found.append(tuple(c % n for c, n in zip(VELOCITY[i], sizes)))
    for stage in STAGES:
        for offset in stage_offsets(stage, sizes):
            found.append(offset)
    return sorted(set(found))


def stage_offsets(stage, sizes):
    result = [(0, 0, 0)]
    for dim, axis in enumerate(AXES):
        if axis in stage:
            result = [
                tuple(k if d == dim else o[d] for d in range(3))
                for o in result
                for k in range(sizes[dim])
            ]
    return [o for o in result if o != (0, 0, 0)]


WALLS = []
for first, s in enumerate(SIGNS):
    WALLS.append(("x", first, 0, (s, 0, 0)))
    WALLS.append(("y", first, 0, (0, s, 0)))
    WALLS.append(("z", first, 0, (0, 0, s)))
    for second, t in enumerate(SIGNS):
        WALLS.append(("xz", first, second, (s, 0, t)))
        WALLS.append(("yx", first, second, (t, s, 0)))


def wall_offsets(sizes):
    return sorted({tuple(c % n for c, n in zip(w[3], sizes)) for w in WALLS})


def kernel(
    sizes,
    pops_in,
    solid_in,
    cell_in,
    panel_in,
    area_in,
    shapes_in,
    panel_mode_in,
    compliance_in,
    out,
    force_out,
    amp_out,
    pops,
    solid,
    cell,
    panel,
    area,
    shape_rows,
    panel_mode,
    compliance,
    mine,
    load_sem,
    post,
    dens,
    wall,
    xs,
    xh,
    wxh,
    ys,
    yh,
    yxh,
    yzh,
    theirs,
    picks,
    surf_send,
    surf_recv,
    slots_a,
    slots_b,
    send_sem,
    recv_sem,
    send_a,
    recv_a,
    send_b,
    recv_b,
):
    depth, rows, width = pops.shape[1:]
    cells = depth * rows
    here = tuple(lax.axis_index(a) for a in AXES)

    def at(offset):
        return tuple(lax.rem(h + o % n, n) if o % n else h for h, o, n in zip(here, offset, sizes))

    partners = offsets_of(sizes)
    barrier = pltpu.get_barrier_semaphore()
    for offset in partners:
        pl.semaphore_signal(barrier, inc=1, device_id=at(offset), device_id_type=MESH)

    pairs = [(cell_in, cell), (panel_in, panel), (area_in, area)]
    pairs += [(solid_in, solid), (shapes_in, shape_rows)]
    pairs += [(panel_mode_in, panel_mode), (compliance_in, compliance)]
    part = depth // N_LOADS
    cuts = [pl.ds(n * part, part) for n in range(N_LOADS)]
    pairs = pairs[:3] + [(pops_in.at[:, c], pops.at[:, c]) for c in cuts] + pairs[3:]
    loads = []
    for n, (src, dst) in enumerate(pairs):
        loads.append(pltpu.make_async_copy(src, dst, load_sem.at[n]))
        loads[n].start()

    lane = lax.broadcasted_iota(jnp.int32, (rows, width), 1)
    sub = lax.broadcasted_iota(jnp.int32, (rows, width), 0)

    for copy in loads[:3]:
        copy.wait()
    live = panel[...] >= 0
    col = lax.rem(cell[...], width)
    row = lax.div(cell[...], width)
    n_surf = cell.shape[1]
    pick_col = jnp.where(
        lax.broadcasted_iota(jnp.int32, (width, n_surf), 0) == col, 1.0, 0.0
    ).astype(BF16)
    on_row = lax.broadcasted_iota(jnp.int32, (cells, n_surf), 0) == row

    def add_up(z, carry):
        density = pops[0, z]
        for i in range(1, 19):
            density = density + pops[i, z]
        dens[z + 1] = density
        return carry

    for n in range(N_LOADS):
        loads[3 + n].wait()
        lax.fori_loop(n * part, (n + 1) * part, add_up, 0, unroll=True)
    gauge_high, gauge_low = halves(dens[pl.ds(1, depth)].reshape(cells, width) - 1.0)
    by_row = dot(gauge_high, pick_col) + dot(gauge_low, pick_col)
    excess = jnp.sum(jnp.where(on_row, by_row, 0.0), axis=0, keepdims=True)
    contrib = jnp.where(live, area[...] * (excess / 3.0), 0.0)
    pick_panel = jnp.where(
        lax.broadcasted_iota(jnp.int32, (width, n_surf), 0) == panel[...], 1.0, 0.0
    ).astype(BF16)
    contrib_high, contrib_low = halves(jnp.broadcast_to(contrib, (8, n_surf)))
    partial = dot_nt(contrib_high, pick_panel) + dot_nt(contrib_low, pick_panel)
    partial = partial[0:1]

    pl.semaphore_wait(barrier, len(partners))

    def stage_start(stage, slots, send, recv, value):
        index = 0
        for dim, axis in enumerate(AXES):
            if axis in stage:
                index = index * sizes[dim] + here[dim]
        slots[index] = value
        copies = []
        for n, offset in enumerate(stage_offsets(stage, sizes)):
            copy = pltpu.make_async_remote_copy(
                src_ref=slots.at[index],
                dst_ref=slots.at[index],
                send_sem=send.at[n],
                recv_sem=recv.at[n],
                device_id=at(offset),
                device_id_type=MESH,
            )
            copy.start()
            copies.append(copy)
        return copies

    def stage_sum(slots, copies):
        for copy in copies:
            copy.wait()
        total = slots[0]
        for n in range(1, slots.shape[0]):
            total = total + slots[n]
        return total

    copies_a = stage_start(STAGES[0], slots_a, send_a, recv_a, partial)

    for copy in loads[3 + N_LOADS :]:
        copy.wait()
    for m in range(MODES):
        mine[m : m + 1, :] = jnp.where(live, shape_rows[m], 0.0)
    mine[MODES : MODES + 1, :] = cell[...].astype(F32)
    mine[MODES + 1 :, :] = jnp.zeros((mine.shape[0] - MODES - 1, n_surf), F32)
    surfels = []
    for n, offset in enumerate(wall_offsets(sizes)):
        copy = pltpu.make_async_remote_copy(
            src_ref=mine,
            dst_ref=theirs.at[n],
            send_sem=surf_send.at[n],
            recv_sem=surf_recv.at[n],
            device_id=at(offset),
            device_id_type=MESH,
        )
        copy.start()
        surfels.append(copy)

    def collide(z, packed):
        f = [pops[i, z] for i in range(19)]
        density = dens[z + 1]
        inverse = 1.0 / density
        u = []
        for axis in range(3):
            plus, minus = moving(axis, 1), moving(axis, -1)
            total = f[plus[0]] - f[minus[0]]
            for i, j in zip(plus[1:], minus[1:]):
                total = total + (f[i] - f[j])
            u.append(total * inverse)
        base = 1.0 - 1.5 * (u[0] * u[0] + u[1] * u[1] + u[2] * u[2])
        fixed = solid[z] == 1
        scaled = [OMEGA * w * density for w in WEIGHTS]
        new = [None] * 19
        new[0] = jnp.where(fixed, f[0], (1.0 - OMEGA) * f[0] + scaled[0] * base)
        for i in range(1, 19, 2):
            proj = None
            for axis in range(3):
                comp = VELOCITY[i][axis]
                if comp:
                    term = u[axis] if comp == 1 else -u[axis]
                    proj = term if proj is None else proj + term
            even = scaled[i] * (base + 4.5 * (proj * proj))
            odd = scaled[i] * (3.0 * proj)
            new[i] = jnp.where(fixed, f[i + 1], (1.0 - OMEGA) * f[i] + (even + odd))
            new[i + 1] = jnp.where(fixed, f[i], (1.0 - OMEGA) * f[i + 1] + (even - odd))
        for i in range(19):
            post[PLACE[i], z + 1] = new[i]
        packed = list(packed)
        for a in range(2):
            edge = rows - 1 if a == 0 else 0
            for k, i in enumerate(X_GROUP[a]):
                xs[a, k, z] = new[i][edge : edge + 1]
            xs[a, 5, z] = density[edge : edge + 1]
            edge = width - 1 if a == 0 else 0
            for j, value in enumerate([new[i] for i in Y_GROUP[a]] + [density]):
                column = jnp.broadcast_to(value[:, edge : edge + 1], (rows, width))
                packed[a] = jnp.where(lane == j * depth + z, column, packed[a])
        return tuple(packed)

    zero = jnp.zeros((rows, width), F32)
    packed = lax.fori_loop(0, depth, collide, (zero, zero))
    for a in range(2):
        ys[a] = packed[a]

    halo = []

    def send(src, dst, offset):
        copy = pltpu.make_async_remote_copy(
            src_ref=src,
            dst_ref=dst,
            send_sem=send_sem.at[len(halo)],
            recv_sem=recv_sem.at[len(halo)],
            device_id=at(offset),
            device_id_type=MESH,
        )
        copy.start()
        halo.append(copy)
        return copy

    for a, s in enumerate(SIGNS):
        group = Z_GROUP[a]
        first = a * len(group)
        source, target = (depth, 0) if a == 0 else (1, depth + 1)
        send(xs.at[a], xh.at[a, :, pl.ds(1, depth)], (s, 0, 0))
        send(
            post.at[pl.ds(first, len(group)), source],
            post.at[pl.ds(first, len(group)), target],
            (0, 0, s),
        )
        send(dens.at[source], dens.at[target], (0, 0, s))
        send(ys.at[a], yh.at[a], (0, s, 0))
        for b, t in enumerate(SIGNS):
            send(ys.at[a], yxh.at[a, b], (t, s, 0))
            send(ys.at[a], yzh.at[a, b], (0, s, t))
            k = [i for i in range(5) if VELOCITY[X_GROUP[a][i]][2] == t][0]
            source, target = (depth - 1, 0) if b == 0 else (0, depth + 1)
            send(xs.at[a, k, source], xh.at[a, k, target], (s, 0, t))
            send(xs.at[a, 5, source], xh.at[a, 5, target], (s, 0, t))

    mode_id = lax.broadcasted_iota(jnp.int32, (MODES, PANELS), 0)
    diagonal = lax.broadcasted_iota(jnp.int32, (MODES, MODES), 0) == lax.broadcasted_iota(
        jnp.int32, (MODES, MODES), 1
    )
    factor = jnp.sum(jnp.where(diagonal, compliance[...], 0.0), axis=1, keepdims=True)
    drives = panel_mode[...] == mode_id

    load_a = stage_sum(slots_a, copies_a)
    copies_b = stage_start(STAGES[1], slots_b, send_b, recv_b, load_a)
    def arrived(moved):
        columns = []
        for a in range(2):
            face = yh[a] + y_flux[a] if moved else yh[a]
            result = face
            for j, i in enumerate(Y_GROUP[a]):
                cx, _, cz = VELOCITY[i]
                mine = (lane >= j * depth) & (lane < (j + 1) * depth)
                if cx and moved:
                    b = SIGNS.index(cx)
                    edge = pltpu.roll(yxh[a, b] + yx_flux[a][b], cx % rows, 0)
                    whole = pltpu.roll(face, cx % rows, 0)
                    whole = jnp.where(sub == (0 if cx == 1 else rows - 1), edge, whole)
                    result = jnp.where(mine, whole, result)
                if cz and not moved:
                    b = SIGNS.index(cz)
                    whole = pltpu.roll(face, cz % width, 1)
                    wrapped = pltpu.roll(yzh[a, b], (-cz * (depth - 1)) % width, 1)
                    spot = j * depth if cz == 1 else (j + 1) * depth - 1
                    whole = jnp.where(lane == spot, wrapped, whole)
                    result = jnp.where(mine, whole, result)
            columns.append(result)
        return columns

    def finish(moved, z, columns):
        for i in range(19):
            cx, cy, cz = VELOCITY[i]
            if bool(cx) != moved:
                continue
            source = z + 1 - cz
            value = post[PLACE[i], source]
            if cx:
                a = SIGNS.index(cx)
                k = X_GROUP[a].index(i)
                value = value + COEF[i] * wall[source]
                line = xh[a, k, source] + COEF[i] * wxh[a, source]
                value = pltpu.roll(value, cx % rows, 0)
                value = jnp.where(sub == (0 if cx == 1 else rows - 1), line, value)
            if cy:
                a = SIGNS.index(cy)
                j = Y_GROUP[a].index(i)
                value = pltpu.roll(value, cy % width, 1)
                column = jnp.broadcast_to(
                    columns[a][:, j * depth : j * depth + 1], (rows, width)
                )
                value = jnp.where(lane == (0 if cy == 1 else width - 1), column, value)
            out[i, z] = value
        return tuple(pltpu.roll(c, width - 1, 1) for c in columns)

    for copy in halo:
        copy.wait()
    lax.fori_loop(0, depth, functools.partial(finish, False), tuple(arrived(False)))

    for copy in surfels:
        copy.wait()
    masks = []
    places = wall_offsets(sizes)
    spot = lax.broadcasted_iota(jnp.int32, (width, n_surf), 0)
    spot_z = lax.rem(spot, depth)
    row_id = lax.broadcasted_iota(jnp.int32, (rows, n_surf), 0)
    level_id = lax.broadcasted_iota(jnp.int32, (depth, n_surf), 0)
    for index, (kind, a, b, velocity) in enumerate(WALLS):
        offset = places.index(tuple(c % n for c, n in zip(velocity, sizes)))
        cells_of = theirs[offset, MODES : MODES + 1, :].astype(jnp.int32)
        cy = lax.rem(cells_of, width)
        cx = lax.rem(lax.div(cells_of, width), rows)
        cz = lax.div(cells_of, width * rows)
        picked = (spot_z == cz) if kind[0] == "y" else (spot == cy)
        picks[index] = jnp.where(picked, 1.0, 0.0).astype(BF16)
        if kind == "x":
            mask = (level_id == cz) & (cx == (rows - 1 if a == 0 else 0))
        elif kind[0] == "y":
            mask = (row_id == cx) & (cy == (width - 1 if a == 0 else 0))
        else:
            up = a if kind == "z" else b
            mask = (row_id == cx) & (cz == (depth - 1 if up == 0 else 0))
        masks.append((mask, offset))

    force = stage_sum(slots_b, copies_b)[:, :PANELS]
    force_out[...] = force
    amp = factor * jnp.sum(jnp.where(drives, force, 0.0), axis=1, keepdims=True)
    amp_out[...] = jnp.sum(jnp.where(diagonal, amp, 0.0), axis=0, keepdims=True)

    def speed_of(block):
        return WALL_SCALE * jnp.sum(amp * block[:MODES, :], axis=0, keepdims=True)

    high, low = halves(jnp.where(on_row, speed_of(mine[...]), 0.0))
    flux = dot_nt(high, pick_col) + dot_nt(low, pick_col)
    flux = flux.reshape(depth, rows, width) * dens[pl.ds(1, depth)]
    wall[pl.ds(1, depth)] = flux

    speeds = [speed_of(theirs[n]) for n in range(len(surfels))]

    def spread(index, mask, offset):
        high, low = halves(jnp.where(mask, speeds[offset], 0.0))
        return dot_nt(high, picks[index]) + dot_nt(low, picks[index])

    def on_lanes(a, tile, flux):
        result = jnp.zeros_like(tile)
        for j, i in enumerate(Y_GROUP[a]):
            if VELOCITY[i][0]:
                mine_lanes = (lane >= j * depth) & (lane < (j + 1) * depth)
                moved = pltpu.roll(tile, (j - 5) * depth % width, 1)
                result = jnp.where(mine_lanes, COEF[i] * moved * flux, result)
        return result

    y_flux = [None, None]
    yx_flux = [[None, None], [None, None]]
    for index, (kind, a, b, velocity) in enumerate(WALLS):
        mask, offset = masks[index]
        flux = spread(index, mask, offset)
        if kind == "x":
            for z in range(depth):
                wxh[a, z + 1] = flux[z : z + 1] * xh[a, 5, z + 1]
        elif kind == "z":
            slot = 0 if a == 0 else depth + 1
            wall[slot] = flux * dens[slot]
        elif kind == "xz":
            edge = rows - 1 if a == 0 else 0
            slot = 0 if b == 0 else depth + 1
            wxh[a, slot] = flux[edge : edge + 1] * xh[a, 5, slot]
        elif kind == "y":
            y_flux[a] = on_lanes(a, yh[a], flux)
        else:
            yx_flux[a][b] = on_lanes(a, yxh[a, b], flux)

    columns = arrived(True)
    lax.fori_loop(0, depth, functools.partial(finish, True), tuple(columns), unroll=2)


def per_device(sizes, pops, solid, cell, panel, area, shapes, panel_mode, compliance):
    depth, rows, width = pops.shape[1:]
    n_surf = cell.shape[-1]
    count = {a: n for a, n in zip(AXES, sizes)}
    n_a, n_b = (
        functools.reduce(lambda x, y: x * y, [count[a] for a in stage]) for stage in STAGES
    )
    vmem = pl.BlockSpec(memory_space=pltpu.VMEM)
    tile = (rows, width)
    messages = 18 + 6
    n_wall = len(wall_offsets(sizes))
    dma = pltpu.SemaphoreType.DMA
    read, force, amp = pl.pallas_call(
        functools.partial(kernel, sizes),
        out_shape=(
            jax.ShapeDtypeStruct(pops.shape, F32),
            jax.ShapeDtypeStruct((1, PANELS), F32),
            jax.ShapeDtypeStruct((1, MODES), F32),
        ),
        in_specs=[pl.BlockSpec(memory_space=pltpu.HBM)] * 8,
        out_specs=(vmem,) * 3,
        scratch_shapes=[
            pltpu.VMEM(pops.shape, F32),
            pltpu.VMEM(solid.shape, jnp.int32),
            pltpu.VMEM((1, n_surf), jnp.int32),
            pltpu.VMEM((1, n_surf), jnp.int32),
            pltpu.VMEM((1, n_surf), F32),
            pltpu.VMEM((MODES, 1, n_surf), F32),
            pltpu.VMEM((1, PANELS), jnp.int32),
            pltpu.VMEM((1, MODES), F32),
            pltpu.VMEM((16, n_surf), F32),
            dma((7 + N_LOADS,)),
            pltpu.VMEM((19, depth + 2) + tile, F32),
            pltpu.VMEM((depth + 2,) + tile, F32),
            pltpu.VMEM((depth + 2,) + tile, F32),
            pltpu.VMEM((2, 6, depth, 1, width), F32),
            pltpu.VMEM((2, 6, depth + 2, 1, width), F32),
            pltpu.VMEM((2, depth + 2, 1, width), F32),
            pltpu.VMEM((2,) + tile, F32),
            pltpu.VMEM((2,) + tile, F32),
            pltpu.VMEM((2, 2) + tile, F32),
            pltpu.VMEM((2, 2) + tile, F32),
            pltpu.VMEM((n_wall, 16, n_surf), F32),
            pltpu.VMEM((len(WALLS), width, n_surf), BF16),
            dma((n_wall,)),
            dma((n_wall,)),
            pltpu.VMEM((n_a, 1, width), F32),
            pltpu.VMEM((n_b, 1, width), F32),
            dma((messages,)),
            dma((messages,)),
            dma((n_a - 1,)),
            dma((n_a - 1,)),
            dma((n_b - 1,)),
            dma((n_b - 1,)),
        ],
        compiler_params=pltpu.CompilerParams(
            collective_id=0, has_side_effects=True, vmem_limit_bytes=32 * 1024 * 1024
        ),
    )(
        *(
            pltpu.with_memory_space_constraint(x, pltpu.HBM)
            for x in (
                pops,
                solid,
                cell.reshape(1, n_surf),
                panel.reshape(1, n_surf),
                area.reshape(1, n_surf),
                shapes.reshape(MODES, 1, n_surf),
                panel_mode.reshape(1, PANELS),
                compliance.reshape(1, MODES),
            )
        )
    )
    return read, force.reshape(PANELS), amp.reshape(MODES)


def solution(mesh):
    placed = (
        P(None, "gz", "gx", "gy"),
        P("gz", "gx", "gy"),
        P("gz", "gx", "gy", None),
        P("gz", "gx", "gy", None),
        P("gz", "gx", "gy", None),
        P("gz", "gx", "gy", None, None),
        P(),
        P(),
    )
    return jax.shard_map(
        functools.partial(per_device, tuple(mesh.shape[a] for a in AXES)),
        mesh=mesh,
        in_specs=placed,
        out_specs=(P(None, "gz", "gx", "gy"), P(), P()),
        check_vma=False,
    )
```

profile of v0, /device:TPU:0, one launch (start us, length us, event | category | flops | bytes accessed | tf_op | source)
XLA Modules:
  0.0 22.1 jit_solution(666234826725314372)
XLA Ops:
  0.6 19.4 %shard_map.103 = (f32[19,16,8,128]{3,2,1,0:T(8,128)S(1)}, f32[1,40]{1,0:T(1,128)S(1)}, f32[1,12]{1,0:T(1,128)S(1)}) custom-call(f32[19,16,8,128]{3,2,1,0:T(8,128)} %pops_in.1, s32[16,8,128]{2,1,0:T(8,128)} %solid_in.1, s32[1,512]{1,0:T(1,128)} %bitcast.11, s32[1,512]{1,0:T(1,128)} %bitcast.12, f32[1,512]{1,0:T(1,128)} %bitcast.13, f32[12,1,512]{2,1,0:T(1,128)} %bitcast.10, ...), custom_call_target="tpu_custom_call" | custom-call | tf_op jit(solution)/shard_map/pallas_call | solution.py:497
  20.0 1.0 %copy.14 = f32[19,16,8,128]{3,2,1,0:T(8,128)} copy(f32[19,16,8,128]{3,2,1,0:T(8,128)S(1)} %get-tuple-element.12) | data formatting | bytes 2490368
  21.1 0.5 %copy.15 = f32[40]{0:T(128)} copy(f32[40]{0:T(128)S(1)} %bitcast.9) | data formatting | bytes 320
  21.6 0.5 %copy.16 = f32[12]{0:T(128)} copy(f32[12]{0:T(128)S(1)} %bitcast.8) | data formatting | bytes 96
where the time goes:
time: 22.3 us; the launch traced here: 22.1 us
  Pallas kernels  19.4 us (87%)
  local copies, waits for them, and re-layouts  2.06 us (9%)
  between operations  0.64 us (3%)
    pallas_call x1, Pallas kernels, per_device(): pl.pallas_call(functools.partial(kernel, sizes), out_shape=(jax.ShapeDtyp...  19.4 us
    unnamed x3, local copies, waits for them, and re-layouts  2.06 us

commit v1 on v0

v1 whole, which is shorter than its diff:
```python
import functools

import jax
import jax.numpy as jnp
from jax import lax
from jax.experimental import pallas as pl
from jax.experimental.pallas import tpu as pltpu
from jax.sharding import PartitionSpec as P

PANELS = 40
MODES = 12
VELOCITY = (
    (0, 0, 0),
    (1, 0, 0),
    (-1, 0, 0),
    (0, 1, 0),
    (0, -1, 0),
    (0, 0, 1),
    (0, 0, -1),
    (1, 1, 0),
    (-1, -1, 0),
    (1, -1, 0),
    (-1, 1, 0),
    (1, 0, 1),
    (-1, 0, -1),
    (1, 0, -1),
    (-1, 0, 1),
    (0, 1, 1),
    (0, -1, -1),
    (0, 1, -1),
    (0, -1, 1),
)
WEIGHTS = (1.0 / 3.0,) + (1.0 / 18.0,) * 6 + (1.0 / 36.0,) * 12
OMEGA = 1.0 / 0.6
WALL_SCALE = 0.02
COEF = tuple(6.0 * w * v[0] for w, v in zip(WEIGHTS, VELOCITY))
SIGNS = (1, -1)


def moving(axis, sign):
    return tuple(i for i in range(19) if VELOCITY[i][axis] == sign)


X_GROUP = tuple(moving(0, s) for s in SIGNS)
Y_GROUP = tuple(moving(1, s) for s in SIGNS)
Z_GROUP = tuple(moving(2, s) for s in SIGNS)
ORDER = Z_GROUP[0] + Z_GROUP[1] + tuple(i for i in range(19) if VELOCITY[i][2] == 0)
PLACE = tuple(ORDER.index(i) for i in range(19))
AXES = ("gx", "gy", "gz")
MESH = pl.DeviceIdType.MESH
N_LOADS = 4
MODE_ROWS = 16
CELL_ROW = MODES
LOW, HIGH = 16, 17
F32 = jnp.float32
BF16 = jnp.bfloat16


def stages_of(sizes):
    if sizes[0] * sizes[1] * sizes[2] <= 64:
        return (AXES,)
    return (("gx",), ("gy", "gz"))


def halves(x):
    high = x.astype(BF16)
    return high, (x - high.astype(F32)).astype(BF16)


def dot(a, b):
    return jnp.dot(a, b, preferred_element_type=F32)


def dot_nt(a, b):
    return lax.dot_general(a, b, (((1,), (1,)), ((), ())), preferred_element_type=F32)


def stage_offsets(stage, sizes):
    result = [(0, 0, 0)]
    for dim, axis in enumerate(AXES):
        if axis in stage:
            result = [
                tuple(k if d == dim else o[d] for d in range(3))
                for o in result
                for k in range(sizes[dim])
            ]
    return [o for o in result if o != (0, 0, 0)]


def offsets_of(sizes):
    found = []
    for i in range(1, 19):
        found.append(tuple(c % n for c, n in zip(VELOCITY[i], sizes)))
    for stage in stages_of(sizes):
        found += stage_offsets(stage, sizes)
    return sorted(set(found))


def tree_sum(terms):
    while len(terms) > 1:
        terms = [sum(terms[k + 1 : k + 2], terms[k]) for k in range(0, len(terms), 2)]
    return terms[0]


N_HALO = 18 + 4
N_SURF = 2 + 4 + 2 + 4 + 2


def exchange(
    sizes,
    pops_in,
    solid_in,
    cell_in,
    panel_in,
    area_in,
    shapes_in,
    panel_mode_in,
    compliance_in,
    pre,
    flux_m,
    flux_x,
    flux_y,
    flux_c,
    total_out,
    drive_out,
    pops,
    solid,
    cell,
    panel,
    area,
    shape_rows,
    panel_mode,
    compliance,
    mine,
    load_sem,
    post,
    dens,
    xs,
    xh,
    ys,
    yh,
    yxh,
    yzh,
    theirs,
    edges,
    edges_in,
    faces,
    faces_in,
    corners,
    corners_in,
    surf_send,
    surf_recv,
    slots,
    send_sem,
    recv_sem,
    stage_send,
    stage_recv,
):
    depth, rows, width = pops.shape[1:]
    cells = depth * rows
    groups = width // depth
    here = tuple(lax.axis_index(a) for a in AXES)
    stages = stages_of(sizes)
    targets = {}

    def at(offset):
        key = tuple(o % n for o, n in zip(offset, sizes))
        if key not in targets:
            targets[key] = tuple(
                lax.rem(h + o, n) if o else h for h, o, n in zip(here, key, sizes)
            )
        return targets[key]

    partners = offsets_of(sizes)
    barrier = pltpu.get_barrier_semaphore()
    for offset in partners:
        pl.semaphore_signal(barrier, inc=1, device_id=at(offset), device_id_type=MESH)

    small = [(cell_in, cell), (panel_in, panel), (area_in, area), (shapes_in, shape_rows)]
    part = depth // N_LOADS
    cuts = [pl.ds(n * part, part) for n in range(N_LOADS)]
    big = [(pops_in.at[:, c], pops.at[:, c]) for c in cuts]
    late = [(solid_in, solid), (panel_mode_in, panel_mode), (compliance_in, compliance)]
    loads = []
    for n, (src, dst) in enumerate(small + big + late):
        loads.append(pltpu.make_async_copy(src, dst, load_sem.at[n]))
        loads[n].start()

    lane = lax.broadcasted_iota(jnp.int32, (rows, width), 1)
    sub = lax.broadcasted_iota(jnp.int32, (rows, width), 0)

    for copy in loads[: len(small)]:
        copy.wait()
    n_surf = cell.shape[1]
    live = panel[...] >= 0
    col = lax.rem(cell[...], width)
    row = lax.div(cell[...], width)
    cell_x = lax.rem(row, rows)
    cell_z = lax.div(row, rows)
    spot = lax.broadcasted_iota(jnp.int32, (width, n_surf), 0)
    pick_col = jnp.where(spot == col, 1.0, 0.0).astype(BF16)
    on_row = lax.broadcasted_iota(jnp.int32, (cells, n_surf), 0) == row

    for m in range(MODES):
        mine[m : m + 1, :] = jnp.where(live, shape_rows[m] * WALL_SCALE, 0.0)
    mine[CELL_ROW : CELL_ROW + 1, :] = cell[...].astype(F32)
    mine[CELL_ROW + 1 :, :] = jnp.zeros((MODE_ROWS - CELL_ROW - 1, n_surf), F32)

    table = mine[...]
    masked = []
    for a in range(2):
        on_x = cell_x == (rows - 1 if a == 0 else 0)
        for b in range(2):
            on_z = cell_z == (depth - 1 if b == 0 else 0)
            masked.append(jnp.where(on_x & on_z, table, 0.0))
    high, low = halves(jnp.concatenate(masked, axis=0))
    edge_rows = dot_nt(high, pick_col) + dot_nt(low, pick_col)
    for k in range(4):
        edges[k // 2, k % 2] = edge_rows[k * MODE_ROWS : (k + 1) * MODE_ROWS]
    row_id = lax.broadcasted_iota(jnp.int32, (rows, n_surf), 0)
    sides = jnp.concatenate(
        [
            jnp.where((row_id == cell_x) & (col == (width - 1 if a == 0 else 0)), 1.0, 0.0)
            for a in range(2)
        ],
        axis=0,
    ).astype(BF16)
    on_z = lax.rem(spot, depth) == cell_z
    for t in range(2):
        spread_rows = jnp.concatenate(
            [
                jnp.broadcast_to(
                    table[t * groups + g : t * groups + g + 1, :]
                    if t * groups + g < MODES
                    else jnp.zeros((1, n_surf), F32),
                    (depth, n_surf),
                )
                for g in range(groups)
            ],
            axis=0,
        )
        high, low = halves(jnp.where(on_z, spread_rows, 0.0))
        packed = dot_nt(sides, high) + dot_nt(sides, low)
        for a in range(2):
            faces[a, t] = packed[a * rows : (a + 1) * rows]
            for b in range(2):
                edge = a * rows + (rows - 1 if b == 0 else 0)
                corners[a, b, t] = packed[edge : edge + 1]

    def add_up(z, carry):
        density = pops[0, z]
        for i in range(1, 19):
            density = density + pops[i, z]
        dens[z] = density
        return carry

    for n in range(N_LOADS):
        loads[len(small) + n].wait()
        lax.fori_loop(n * part, (n + 1) * part, add_up, 0, unroll=True)
    gauge_high, gauge_low = halves(dens[...].reshape(cells, width) - 1.0)
    by_row = dot(gauge_high, pick_col) + dot(gauge_low, pick_col)
    excess = jnp.sum(jnp.where(on_row, by_row, 0.0), axis=0, keepdims=True)
    contrib = jnp.where(live, area[...] * (excess / 3.0), 0.0)
    pick_panel = jnp.where(spot == panel[...], 1.0, 0.0).astype(BF16)
    contrib_high, contrib_low = halves(jnp.broadcast_to(contrib, (8, n_surf)))
    partial = dot_nt(contrib_high, pick_panel) + dot_nt(contrib_low, pick_panel)
    partial = partial[0:1]

    pl.semaphore_wait(barrier, len(partners))

    def stage_start(n, value):
        stage = stages[n]
        index = 0
        for dim, axis in enumerate(AXES):
            if axis in stage:
                index = index * sizes[dim] + here[dim]
        slots[n, index] = value
        for offset in stage_offsets(stage, sizes):
            pltpu.make_async_remote_copy(
                src_ref=slots.at[n, index],
                dst_ref=slots.at[n, index],
                send_sem=stage_send.at[n],
                recv_sem=stage_recv.at[n],
                device_id=at(offset),
                device_id_type=MESH,
            ).start()

    def stage_sum(n):
        count = len(stage_offsets(stages[n], sizes))
        whole = pltpu.make_async_remote_copy(
            src_ref=slots.at[n, pl.ds(0, count)],
            dst_ref=slots.at[n, pl.ds(0, count)],
            send_sem=stage_send.at[n],
            recv_sem=stage_recv.at[n],
            device_id=at(stage_offsets(stages[n], sizes)[0]),
            device_id_type=MESH,
        )
        whole.wait_recv()
        whole.wait_send()
        return tree_sum([slots[n, k] for k in range(count + 1)])

    stage_start(0, partial)

    surfels = []

    def pass_on(src, dst, offset):
        copy = pltpu.make_async_remote_copy(
            src_ref=src,
            dst_ref=dst,
            send_sem=surf_send.at[len(surfels)],
            recv_sem=surf_recv.at[len(surfels)],
            device_id=at(offset),
            device_id_type=MESH,
        )
        copy.start()
        surfels.append(copy)

    for a, s in enumerate(SIGNS):
        pass_on(mine, theirs.at[a], (s, 0, 0))
        pass_on(faces.at[a], faces_in.at[a], (0, s, 0))
        for b, t in enumerate(SIGNS):
            pass_on(edges.at[a, b], edges_in.at[a, b], (s, 0, t))
            pass_on(corners.at[a, b], corners_in.at[a, b], (t, s, 0))

    loads[len(small) + N_LOADS].wait()

    def collide(z, packed):
        f = [pops[i, z] for i in range(19)]
        density = dens[z]
        inverse = 1.0 / density
        u = []
        for axis in range(3):
            plus, minus = moving(axis, 1), moving(axis, -1)
            total = f[plus[0]] - f[minus[0]]
            for i, j in zip(plus[1:], minus[1:]):
                total = total + (f[i] - f[j])
            u.append(total * inverse)
        base = 1.0 - 1.5 * (u[0] * u[0] + u[1] * u[1] + u[2] * u[2])
        fixed = solid[z] == 1
        scaled = [OMEGA * w * density for w in WEIGHTS]
        new = [None] * 19
        new[0] = jnp.where(fixed, f[0], (1.0 - OMEGA) * f[0] + scaled[0] * base)
        for i in range(1, 19, 2):
            proj = None
            for axis in range(3):
                comp = VELOCITY[i][axis]
                if comp:
                    term = u[axis] if comp == 1 else -u[axis]
                    proj = term if proj is None else proj + term
            even = scaled[i] * (base + 4.5 * (proj * proj))
            odd = scaled[i] * (3.0 * proj)
            new[i] = jnp.where(fixed, f[i + 1], (1.0 - OMEGA) * f[i] + (even + odd))
            new[i + 1] = jnp.where(fixed, f[i], (1.0 - OMEGA) * f[i + 1] + (even - odd))
        for i in range(19):
            post[PLACE[i], z + 1] = new[i]
        packed = list(packed)
        for a in range(2):
            edge = rows - 1 if a == 0 else 0
            for k, i in enumerate(X_GROUP[a]):
                xs[a, k, z] = new[i][edge : edge + 1]
            xs[a, 5, z] = density[edge : edge + 1]
            edge = width - 1 if a == 0 else 0
            for j, value in enumerate([new[i] for i in Y_GROUP[a]] + [density]):
                column = jnp.broadcast_to(value[:, edge : edge + 1], (rows, width))
                packed[a] = jnp.where(lane == j * depth + z, column, packed[a])
        return tuple(packed)

    zero = jnp.zeros((rows, width), F32)
    packed = lax.fori_loop(0, depth, collide, (zero, zero))
    for a in range(2):
        ys[a] = packed[a]

    halo = []

    def send(src, dst, offset):
        copy = pltpu.make_async_remote_copy(
            src_ref=src,
            dst_ref=dst,
            send_sem=send_sem.at[len(halo)],
            recv_sem=recv_sem.at[len(halo)],
            device_id=at(offset),
            device_id_type=MESH,
        )
        copy.start()
        halo.append(copy)

    for a, s in enumerate(SIGNS):
        group = Z_GROUP[a]
        first = a * len(group)
        source, target = (depth, 0) if a == 0 else (1, depth + 1)
        send(xs.at[a], xh.at[a, :, pl.ds(1, depth)], (s, 0, 0))
        send(ys.at[a], yh.at[a], (0, s, 0))
        for b, t in enumerate(SIGNS):
            send(ys.at[a], yxh.at[a, b], (t, s, 0))
            send(ys.at[a], yzh.at[a, b], (0, s, t))
            k = [i for i in range(5) if VELOCITY[X_GROUP[a][i]][2] == t][0]
            edge, beyond = (depth - 1, 0) if b == 0 else (0, depth + 1)
            send(xs.at[a, k, edge], xh.at[a, k, beyond], (s, 0, t))
            send(xs.at[a, 5, edge], xh.at[a, 5, beyond], (s, 0, t))
        send(
            post.at[pl.ds(first, len(group)), source],
            post.at[pl.ds(first, len(group)), target],
            (0, 0, s),
        )

    in_row = jnp.where(on_row, 1.0, 0.0).astype(BF16).reshape(cells // 16, 16, n_surf)

    def scatter(m, carry):
        high, low = halves(jnp.broadcast_to(mine[pl.ds(m, 1), :], (16, n_surf)))
        flux = dot_nt((in_row * high[None]).reshape(cells, n_surf), pick_col)
        flux = flux + dot_nt((in_row * low[None]).reshape(cells, n_surf), pick_col)
        flux_m[m, pl.ds(1, depth)] = flux.reshape(depth, rows, width) * dens[...]
        return carry

    lax.fori_loop(0, MODES, scatter, 0)
    for a, s in enumerate(SIGNS):
        source, target = (depth, 0) if a == 0 else (1, depth + 1)
        pass_on(flux_m.at[:, source], flux_m.at[:, target], (0, 0, s))

    for copy in loads[len(small) + N_LOADS + 1 :]:
        copy.wait()
    mode_id = lax.broadcasted_iota(jnp.int32, (MODE_ROWS, PANELS), 0)
    diagonal = lax.broadcasted_iota(jnp.int32, (MODE_ROWS, MODES), 0) == lax.broadcasted_iota(
        jnp.int32, (MODE_ROWS, MODES), 1
    )
    factor = jnp.sum(jnp.where(diagonal, compliance[...], 0.0), axis=1, keepdims=True)
    drive_out[...] = jnp.where(panel_mode[...] == mode_id, factor, 0.0)

    for n in range(1, len(stages)):
        stage_start(n, stage_sum(n - 1))

    for copy in halo:
        copy.wait()

    columns = []
    for a in range(2):
        result = yh[a]
        for j, i in enumerate(Y_GROUP[a]):
            cx, _, cz = VELOCITY[i]
            own = (lane >= j * depth) & (lane < (j + 1) * depth)
            if cx:
                b = SIGNS.index(cx)
                edge = pltpu.roll(yxh[a, b], cx % rows, 0)
                whole = pltpu.roll(yh[a], cx % rows, 0)
                whole = jnp.where(sub == (0 if cx == 1 else rows - 1), edge, whole)
                result = jnp.where(own, whole, result)
            if cz:
                b = SIGNS.index(cz)
                whole = pltpu.roll(yh[a], cz % width, 1)
                wrapped = pltpu.roll(yzh[a, b], (-cz * (depth - 1)) % width, 1)
                place = j * depth if cz == 1 else (j + 1) * depth - 1
                whole = jnp.where(lane == place, wrapped, whole)
                result = jnp.where(own, whole, result)
        columns.append(result)

    def stream(z, columns):
        for i in range(19):
            cx, cy, cz = VELOCITY[i]
            source = z + 1 - cz
            value = post[PLACE[i], source]
            if cx:
                a = SIGNS.index(cx)
                line = xh[a, X_GROUP[a].index(i), source]
                value = pltpu.roll(value, cx % rows, 0)
                value = jnp.where(sub == (0 if cx == 1 else rows - 1), line, value)
            if cy:
                a = SIGNS.index(cy)
                j = Y_GROUP[a].index(i)
                value = pltpu.roll(value, cy % width, 1)
                column = jnp.broadcast_to(
                    columns[a][:, j * depth : j * depth + 1], (rows, width)
                )
                value = jnp.where(lane == (0 if cy == 1 else width - 1), column, value)
            pre[i, z] = value
        return tuple(pltpu.roll(c, width - 1, 1) for c in columns)

    lax.fori_loop(0, depth, stream, tuple(columns), unroll=2)

    for copy in surfels:
        copy.wait()

    def everywhere(tile, group):
        tile = jnp.where(lane // depth == group, tile, 0.0)
        step = depth
        while step < width:
            tile = tile + pltpu.roll(tile, step, 1)
            step *= 2
        return tile

    level_id = lax.broadcasted_iota(jnp.int32, (depth, n_surf), 0)
    for a in range(2):
        other = theirs[a, CELL_ROW : CELL_ROW + 1, :].astype(jnp.int32)
        pick = jnp.where(spot == lax.rem(other, width), 1.0, 0.0).astype(BF16)
        on_x = lax.rem(lax.div(other, width), rows) == (rows - 1 if a == 0 else 0)
        on_face = (level_id == lax.div(other, width * rows)) & on_x
        lines = jnp.concatenate(
            [jnp.where(on_face, theirs[a, m : m + 1, :], 0.0) for m in range(MODES)], axis=0
        )
        high, low = halves(lines)
        lines = dot_nt(high, pick) + dot_nt(low, pick)
        density = xh[a, 5, pl.ds(1, depth)].reshape(depth, width)
        for m in range(MODES):
            flux_x[a, m, 0:depth, :] = lines[m * depth : (m + 1) * depth] * density
        for b in range(2):
            place, slot = (LOW, 0) if b == 0 else (HIGH, depth + 1)
            line = xh[a, 5, slot]
            for m in range(MODES):
                flux_x[a, m, place : place + 1, :] = edges_in[a, b, m : m + 1, :] * line
        density = everywhere(yh[a], 5)
        for t in range(2):
            flux_y[a, t] = faces_in[a, t] * density
        for b in range(2):
            density = everywhere(yxh[a, b], 5)
            edge = rows - 1 if b == 0 else 0
            for t in range(2):
                k = 2 * a + b
                flux_c[t, k : k + 1, :] = corners_in[a, b, t] * density[edge : edge + 1]
    flux_c[:, 4:, :] = jnp.zeros((2, rows - 4, width), F32)
    for a in range(2):
        for m in range(MODES):
            flux_x[a, m, HIGH + 1 :, :] = jnp.zeros((rows - 2, width), F32)

    total_out[...] = stage_sum(len(stages) - 1)


MOVED = X_GROUP[0] + X_GROUP[1]
FIXED_RUNS = ((0, 1), (3, 4), (15, 4))
MOVED_RUNS = ((1, 2), (7, 8))
N_CUTS = 4


def apply(pre, flux_m, flux_x, flux_y, flux_c, total, drive, out, force_out, amp_out, stage, force, amplitude, sem):
    depth, rows, width = pre.shape[1:]
    copies = []

    def write(src, dst):
        copy = pltpu.make_async_copy(src, dst, sem.at[len(copies)])
        copy.start()
        copies.append(copy)

    for first, count in FIXED_RUNS:
        run = pl.ds(first, count)
        write(pre.at[run], out.at[run])

    lane = lax.broadcasted_iota(jnp.int32, (rows, width), 1)
    sub = lax.broadcasted_iota(jnp.int32, (rows, width), 0)
    load = total[:, :PANELS]
    force[...] = load
    write(force, force_out)
    amp = jnp.sum(drive[...] * load, axis=1, keepdims=True)
    diagonal = lax.broadcasted_iota(jnp.int32, (MODE_ROWS, MODES), 0) == lax.broadcasted_iota(
        jnp.int32, (MODE_ROWS, MODES), 1
    )
    amps = [jnp.broadcast_to(amp[m : m + 1], (rows, width)) for m in range(MODES)]
    groups = width // depth
    gains = []
    for t in range(2):
        gain = jnp.zeros((rows, width), F32)
        for m in range(t * groups, min(MODES, (t + 1) * groups)):
            gain = jnp.where(lane // depth == m - t * groups, amps[m], gain)
        gains.append(gain)

    def gather(first, second):
        tile = first * gains[0] + second * gains[1]
        step = depth
        while step < width:
            tile = tile + pltpu.roll(tile, step, 1)
            step *= 2
        return tile

    corner = gather(flux_c[0], flux_c[1])
    columns = {}
    for a, s in enumerate(SIGNS):
        face = gather(flux_y[a, 0], flux_y[a, 1])
        for b, t in enumerate(SIGNS):
            edge = corner[2 * a + b : 2 * a + b + 1]
            moved = pltpu.roll(face, t % rows, 0)
            columns[t, s] = jnp.where(sub == (0 if t == 1 else rows - 1), edge, moved)

    def weigh(terms):
        return tree_sum([amps[m] * terms[m] for m in range(MODES)])

    lines = [
        [
            weigh([flux_x[a, m, r * rows : (r + 1) * rows, :] for m in range(MODES)])
            for r in range(3)
        ]
        for a in range(2)
    ]

    def put(i, z, value):
        stage[i, z] = pre[i, z] + COEF[i] * value

    part = depth // N_CUTS
    for slot in range(depth + 2):
        flux = weigh([flux_m[m, slot] for m in range(MODES)])
        place = LOW if slot == 0 else HIGH if slot == depth + 1 else slot - 1
        for a, s in enumerate(SIGNS):
            line = lines[a][place // rows][place % rows : place % rows + 1]
            moved = pltpu.roll(flux, s % rows, 0)
            moved = jnp.where(sub == (0 if s == 1 else rows - 1), line, moved)
            for i in X_GROUP[a]:
                _, cy, cz = VELOCITY[i]
                z = slot - 1 + cz
                if not 0 <= z < depth:
                    continue
                value = moved
                if cy:
                    value = pltpu.roll(moved, cy % width, 1)
                    column = jnp.broadcast_to(columns[s, cy][:, z : z + 1], (rows, width))
                    value = jnp.where(lane == (0 if cy == 1 else width - 1), column, value)
                put(i, z, value)
        if slot >= 2 and (slot - 1) % part == 0:
            cut = pl.ds(slot - 1 - part, part)
            for first, count in MOVED_RUNS:
                run = pl.ds(first, count)
                write(stage.at[run, cut], out.at[run, cut])
    amplitude[...] = jnp.sum(jnp.where(diagonal, amp, 0.0), axis=0, keepdims=True)
    write(amplitude, amp_out)
    for copy in copies:
        copy.wait()


def per_device(sizes, pops, solid, cell, panel, area, shapes, panel_mode, compliance):
    depth, rows, width = pops.shape[1:]
    n_surf = cell.shape[-1]
    stages = stages_of(sizes)
    n_slots = max(len(stage_offsets(stage, sizes)) + 1 for stage in stages)
    vmem = pl.BlockSpec(memory_space=pltpu.VMEM)
    hbm = pl.BlockSpec(memory_space=pltpu.HBM)
    tile = (rows, width)
    dma = pltpu.SemaphoreType.DMA
    passed = pl.pallas_call(
        functools.partial(exchange, sizes),
        out_shape=(
            jax.ShapeDtypeStruct(pops.shape, F32),
            jax.ShapeDtypeStruct((MODES, depth + 2) + tile, F32),
            jax.ShapeDtypeStruct((2, MODES, depth + rows, width), F32),
            jax.ShapeDtypeStruct((2, 2) + tile, F32),
            jax.ShapeDtypeStruct((2,) + tile, F32),
            jax.ShapeDtypeStruct((1, width), F32),
            jax.ShapeDtypeStruct((MODE_ROWS, PANELS), F32),
        ),
        in_specs=[hbm] * 8,
        out_specs=(vmem,) * 7,
        scratch_shapes=[
            pltpu.VMEM(pops.shape, F32),
            pltpu.VMEM(solid.shape, jnp.int32),
            pltpu.VMEM((1, n_surf), jnp.int32),
            pltpu.VMEM((1, n_surf), jnp.int32),
            pltpu.VMEM((1, n_surf), F32),
            pltpu.VMEM((MODES, 1, n_surf), F32),
            pltpu.VMEM((1, PANELS), jnp.int32),
            pltpu.VMEM((1, MODES), F32),
            pltpu.VMEM((MODE_ROWS, n_surf), F32),
            dma((7 + N_LOADS,)),
            pltpu.VMEM((19, depth + 2) + tile, F32),
            pltpu.VMEM((depth,) + tile, F32),
            pltpu.VMEM((2, 6, depth, 1, width), F32),
            pltpu.VMEM((2, 6, depth + 2, 1, width), F32),
            pltpu.VMEM((2,) + tile, F32),
            pltpu.VMEM((2,) + tile, F32),
            pltpu.VMEM((2, 2) + tile, F32),
            pltpu.VMEM((2, 2) + tile, F32),
            pltpu.VMEM((2, MODE_ROWS, n_surf), F32),
            pltpu.VMEM((2, 2, MODE_ROWS, width), F32),
            pltpu.VMEM((2, 2, MODE_ROWS, width), F32),
            pltpu.VMEM((2, 2) + tile, F32),
            pltpu.VMEM((2, 2) + tile, F32),
            pltpu.VMEM((2, 2, 2, 1, width), F32),
            pltpu.VMEM((2, 2, 2, 1, width), F32),
            dma((N_SURF,)),
            dma((N_SURF,)),
            pltpu.VMEM((len(stages), n_slots, 1, width), F32),
            dma((N_HALO,)),
            dma((N_HALO,)),
            dma((len(stages),)),
            dma((len(stages),)),
        ],
        compiler_params=pltpu.CompilerParams(
            collective_id=0, has_side_effects=True, vmem_limit_bytes=24 * 1024 * 1024
        ),
    )(
        *(
            pltpu.with_memory_space_constraint(x, pltpu.HBM)
            for x in (
                pops,
                solid,
                cell.reshape(1, n_surf),
                panel.reshape(1, n_surf),
                area.reshape(1, n_surf),
                shapes.reshape(MODES, 1, n_surf),
                panel_mode.reshape(1, PANELS),
                compliance.reshape(1, MODES),
            )
        )
    )
    read, force, amp = pl.pallas_call(
        apply,
        out_shape=(
            jax.ShapeDtypeStruct(pops.shape, F32),
            jax.ShapeDtypeStruct((1, PANELS), F32),
            jax.ShapeDtypeStruct((1, MODES), F32),
        ),
        in_specs=[vmem] * 7,
        out_specs=(hbm,) * 3,
        scratch_shapes=[
            pltpu.VMEM(pops.shape, F32),
            pltpu.VMEM((1, PANELS), F32),
            pltpu.VMEM((1, MODES), F32),
            dma((len(FIXED_RUNS) + len(MOVED_RUNS) * N_CUTS + 2,)),
        ],
        compiler_params=pltpu.CompilerParams(vmem_limit_bytes=8 * 1024 * 1024),
    )(*passed)
    return read, force.reshape(PANELS), amp.reshape(MODES)


def solution(mesh):
    placed = (
        P(None, "gz", "gx", "gy"),
        P("gz", "gx", "gy"),
        P("gz", "gx", "gy", None),
        P("gz", "gx", "gy", None),
        P("gz", "gx", "gy", None),
        P("gz", "gx", "gy", None, None),
        P(),
        P(),
    )
    return jax.shard_map(
        functools.partial(per_device, tuple(mesh.shape[a] for a in AXES)),
        mesh=mesh,
        in_specs=placed,
        out_specs=(P(None, "gz", "gx", "gy"), P(), P()),
        check_vma=False,
    )
```

time: 22.3 us -> 18.4 us (0.83)
  local copies, waits for them, and re-layouts: 2.06 us -> 0 us
  Pallas kernels: 19.4 us -> 17.6 us
    unnamed x3 -> x0, local copies, waits for them, and re-layouts: 2.06 us -> none
    pallas_call x1 -> x2, Pallas kernels: 19.4 us -> 17.6 us  [the longest x1 16.2 us: per_device(): pl.pallas_call(functools.partial(exchange, sizes), out_shape=(jax.ShapeDt...]
where the time goes in v1:
time: 18.4 us; the launch traced here: 18.2 us
  Pallas kernels  17.6 us (96%)
  between operations  0.64 us (3%)
    pallas_call x1, Pallas kernels, per_device(): pl.pallas_call(functools.partial(exchange, sizes), out_shape=(jax.ShapeDt...  16.2 us
    pallas_call x1, Pallas kernels, per_device(): pl.pallas_call(apply, out_shape=(jax.ShapeDtypeStruct(pops.shape, F32), j...  1.37 us

profile of v1, /device:TPU:0, one launch (start us, length us, event | category | flops | bytes accessed | tf_op | source)
XLA Modules:
  0.0 18.2 jit_solution(15984310228250806559)
XLA Ops:
  0.6 16.2 %shard_map.103 = (f32[19,16,8,128]{3,2,1,0:T(8,128)S(1)}, f32[12,18,8,128]{3,2,1,0:T(8,128)S(1)}, f32[2,12,24,128]{3,2,1,0:T(8,128)S(1)}, f32[2,2,8,128]{3,2,1,0...) custom-call(f32[19,16,8,128]{3,2,1,0:T(8,128)} %pops_in.1, ...), custom_call_target="tpu_custom_call" | custom-call | tf_op jit(solution)/shard_map/pallas_call | solution.py:633
  16.8 1.4 %shard_map.104 = (f32[19,16,8,128]{3,2,1,0:T(8,128)}, f32[1,40]{1,0:T(1,128)}, f32[1,12]{1,0:T(1,128)}) custom-call(f32[19,16,8,128]{3,2,1,0:T(8,128)S(1)} %get-tuple-element.13.pre, f32[12,18,8,128]{3,2,1,0:T(8,128)S(1)} %get-tuple-element.14.flux_m, f32[2,12,24,128]{3,2,1,0:T(8,128)S(1)} %get-tuple-element.15.flux_x, ...), custom_call_target="tpu_custom_call" | custom-call | tf_op jit(solution)/shard_map/pallas_call | solution.py:698

commit v2 on v1

--- a/solution.py
+++ b/solution.py
@@ -102,7 +102,8 @@
     return terms[0]
 
 
-N_HALO = 18 + 4
+N_HALO = 18
+PER_DOT = 2
 N_SURF = 2 + 4 + 2 + 4 + 2
 
 
@@ -121,6 +122,7 @@
     flux_x,
     flux_y,
     flux_c,
+    column_out,
     total_out,
     drive_out,
     pops,
@@ -133,13 +135,15 @@
     compliance,
     mine,
     load_sem,
-    post,
     dens,
     xs,
     xh,
+    xe,
+    xeh,
     ys,
     yh,
-    yxh,
+    yr,
+    yrh,
     yzh,
     theirs,
     edges,
@@ -201,12 +205,13 @@
     pick_col = jnp.where(spot == col, 1.0, 0.0).astype(BF16)
     on_row = lax.broadcasted_iota(jnp.int32, (cells, n_surf), 0) == row
 
-    for m in range(MODES):
-        mine[m : m + 1, :] = jnp.where(live, shape_rows[m] * WALL_SCALE, 0.0)
-    mine[CELL_ROW : CELL_ROW + 1, :] = cell[...].astype(F32)
-    mine[CELL_ROW + 1 :, :] = jnp.zeros((MODE_ROWS - CELL_ROW - 1, n_surf), F32)
-
-    table = mine[...]
+    table = [jnp.where(live, shape_rows[m] * WALL_SCALE, 0.0) for m in range(MODES)]
+    table.append(cell[...].astype(F32))
+    for m, line in enumerate(table):
+        mine[m] = line
+    table = jnp.concatenate(
+        table[:MODES] + [jnp.zeros((MODE_ROWS - MODES, n_surf), F32)], axis=0
+    )
     masked = []
     for a in range(2):
         on_x = cell_x == (rows - 1 if a == 0 else 0)
@@ -251,13 +256,13 @@
         density = pops[0, z]
         for i in range(1, 19):
             density = density + pops[i, z]
-        dens[z] = density
+        dens[pl.ds(pl.multiple_of(z * rows, rows), rows)] = density
         return carry
 
     for n in range(N_LOADS):
         loads[len(small) + n].wait()
         lax.fori_loop(n * part, (n + 1) * part, add_up, 0, unroll=True)
-    gauge_high, gauge_low = halves(dens[...].reshape(cells, width) - 1.0)
+    gauge_high, gauge_low = halves(dens[...] - 1.0)
     by_row = dot(gauge_high, pick_col) + dot(gauge_low, pick_col)
     excess = jnp.sum(jnp.where(on_row, by_row, 0.0), axis=0, keepdims=True)
     contrib = jnp.where(live, area[...] * (excess / 3.0), 0.0)
@@ -326,7 +331,7 @@
 
     def collide(z, packed):
         f = [pops[i, z] for i in range(19)]
-        density = dens[z]
+        density = dens[pl.ds(pl.multiple_of(z * rows, rows), rows)]
         inverse = 1.0 / density
         u = []
         for axis in range(3):
@@ -351,23 +356,51 @@
             odd = scaled[i] * (3.0 * proj)
             new[i] = jnp.where(fixed, f[i + 1], (1.0 - OMEGA) * f[i] + (even + odd))
             new[i + 1] = jnp.where(fixed, f[i], (1.0 - OMEGA) * f[i + 1] + (even - odd))
+        packed = list(packed)
+
+        def pack(a, value, edge, place):
+            column = jnp.broadcast_to(value[:, edge : edge + 1], (rows, width))
+            packed[a] = jnp.where(lane == place, column, packed[a])
+
         for i in range(19):
-            post[PLACE[i], z + 1] = new[i]
-        packed = list(packed)
+            cx, cy, cz = VELOCITY[i]
+            value = new[i]
+            if cx:
+                value = pltpu.roll(value, cx % rows, 0)
+            if cy:
+                value = pltpu.roll(value, cy % width, 1)
+                a = SIGNS.index(cy)
+                place = z if cz == 0 else lax.rem(z + cz + depth, depth)
+                edge = 0 if cy == 1 else width - 1
+                pack(a, value, edge, Y_GROUP[a].index(i) * depth + place)
+            pre[PLACE[i], pl.ds(pl.multiple_of((z + 1 + cz) * rows, rows), rows)] = value
         for a in range(2):
-            edge = rows - 1 if a == 0 else 0
-            for k, i in enumerate(X_GROUP[a]):
-                xs[a, k, z] = new[i][edge : edge + 1]
-            xs[a, 5, z] = density[edge : edge + 1]
-            edge = width - 1 if a == 0 else 0
-            for j, value in enumerate([new[i] for i in Y_GROUP[a]] + [density]):
-                column = jnp.broadcast_to(value[:, edge : edge + 1], (rows, width))
-                packed[a] = jnp.where(lane == j * depth + z, column, packed[a])
+            pack(a, density, width - 1 if a == 0 else 0, 5 * depth + z)
         return tuple(packed)
 
     zero = jnp.zeros((rows, width), F32)
     packed = lax.fori_loop(0, depth, collide, (zero, zero))
+    line_lane = lax.broadcasted_iota(jnp.int32, (1, width), 1)
     for a in range(2):
+        wrap, edge = (0, rows - 1) if a == 0 else (rows - 1, 0)
+        for k, i in enumerate(X_GROUP[a]):
+            cz = VELOCITY[i][2]
+            first = (1 + cz) * rows + wrap
+            xs[a, k] = pre[PLACE[i], pl.ds(first, depth, stride=rows), :]
+            if cz:
+                b = SIGNS.index(cz)
+                first = (depth + 1 if b == 0 else 0) * rows + wrap
+                xe[a, b, 0] = pre[PLACE[i], first : first + 1, :]
+        xs[a, 5] = dens[pl.ds(edge, depth, stride=rows), :]
+        for b in range(2):
+            first = (depth - 1 if b == 0 else 0) * rows + edge
+            xe[a, b, 1] = dens[first : first + 1, :]
+            wrap_b, edge_b = (0, rows - 1) if b == 0 else (rows - 1, 0)
+            yr[a, b] = jnp.where(
+                line_lane < 5 * depth,
+                packed[a][wrap_b : wrap_b + 1],
+                packed[a][edge_b : edge_b + 1],
+            )
         ys[a] = packed[a]
 
     halo = []
@@ -385,34 +418,43 @@
         halo.append(copy)
 
     for a, s in enumerate(SIGNS):
-        group = Z_GROUP[a]
-        first = a * len(group)
-        source, target = (depth, 0) if a == 0 else (1, depth + 1)
-        send(xs.at[a], xh.at[a, :, pl.ds(1, depth)], (s, 0, 0))
+        send(xs.at[a], xh.at[a], (s, 0, 0))
         send(ys.at[a], yh.at[a], (0, s, 0))
         for b, t in enumerate(SIGNS):
-            send(ys.at[a], yxh.at[a, b], (t, s, 0))
+            send(yr.at[a, b], yrh.at[a, b], (t, s, 0))
             send(ys.at[a], yzh.at[a, b], (0, s, t))
-            k = [i for i in range(5) if VELOCITY[X_GROUP[a][i]][2] == t][0]
-            edge, beyond = (depth - 1, 0) if b == 0 else (0, depth + 1)
-            send(xs.at[a, k, edge], xh.at[a, k, beyond], (s, 0, t))
-            send(xs.at[a, 5, edge], xh.at[a, 5, beyond], (s, 0, t))
+            send(xe.at[a, b], xeh.at[a, b], (s, 0, t))
+        group = pl.ds(a * 5, 5)
+        source, target = (depth + 1, 1) if a == 0 else (0, depth)
         send(
-            post.at[pl.ds(first, len(group)), source],
-            post.at[pl.ds(first, len(group)), target],
+            pre.at[group, pl.ds(source * rows, rows)],
+            pre.at[group, pl.ds(target * rows, rows)],
             (0, 0, s),
         )
 
-    in_row = jnp.where(on_row, 1.0, 0.0).astype(BF16).reshape(cells // 16, 16, n_surf)
-
-    def scatter(m, carry):
-        high, low = halves(jnp.broadcast_to(mine[pl.ds(m, 1), :], (16, n_surf)))
-        flux = dot_nt((in_row * high[None]).reshape(cells, n_surf), pick_col)
-        flux = flux + dot_nt((in_row * low[None]).reshape(cells, n_surf), pick_col)
-        flux_m[m, pl.ds(1, depth)] = flux.reshape(depth, rows, width) * dens[...]
+    half = cells // 2
+    in_row = lax.broadcasted_iota(jnp.int32, (half, n_surf), 0) == lax.rem(row, half)
+    in_row = jnp.where(in_row, 1.0, 0.0).astype(BF16).reshape(half // 16, 16, n_surf)
+    wide = lax.broadcasted_iota(jnp.int32, (2 * width, n_surf), 0)
+    pick_half = jnp.where(wide == lax.div(row, half) * width + col, 1.0, 0.0).astype(BF16)
+
+    def scatter(step, carry):
+        parts = []
+        for k in range(PER_DOT):
+            line = jnp.broadcast_to(mine[step * PER_DOT + k], (16, n_surf))
+            for value in halves(line):
+                parts.append((in_row * value[None]).reshape(half, n_surf))
+        found = dot_nt(jnp.concatenate(parts, axis=0), pick_half)
+        for k in range(PER_DOT):
+            first = 2 * k * half
+            flux = found[first : first + half] + found[first + half : first + 2 * half]
+            for h in range(2):
+                value = flux[:, h * width : (h + 1) * width] * dens[h * half : (h + 1) * half]
+                value = value.reshape(depth // 2, rows, width)
+                flux_m[step * PER_DOT + k, pl.ds(1 + h * (depth // 2), depth // 2)] = value
         return carry
 
-    lax.fori_loop(0, MODES, scatter, 0)
+    lax.fori_loop(0, MODES // PER_DOT, scatter, 0)
     for a, s in enumerate(SIGNS):
         source, target = (depth, 0) if a == 0 else (1, depth + 1)
         pass_on(flux_m.at[:, source], flux_m.at[:, target], (0, 0, s))
@@ -437,44 +479,33 @@
         result = yh[a]
         for j, i in enumerate(Y_GROUP[a]):
             cx, _, cz = VELOCITY[i]
-            own = (lane >= j * depth) & (lane < (j + 1) * depth)
             if cx:
-                b = SIGNS.index(cx)
-                edge = pltpu.roll(yxh[a, b], cx % rows, 0)
-                whole = pltpu.roll(yh[a], cx % rows, 0)
-                whole = jnp.where(sub == (0 if cx == 1 else rows - 1), edge, whole)
-                result = jnp.where(own, whole, result)
+                own = (lane >= j * depth) & (lane < (j + 1) * depth)
+                own = own & (sub == (0 if cx == 1 else rows - 1))
+                result = jnp.where(own, yrh[a, SIGNS.index(cx)], result)
             if cz:
-                b = SIGNS.index(cz)
-                whole = pltpu.roll(yh[a], cz % width, 1)
-                wrapped = pltpu.roll(yzh[a, b], (-cz * (depth - 1)) % width, 1)
                 place = j * depth if cz == 1 else (j + 1) * depth - 1
-                whole = jnp.where(lane == place, wrapped, whole)
-                result = jnp.where(own, whole, result)
+                result = jnp.where(lane == place, yzh[a, SIGNS.index(cz)], result)
         columns.append(result)
-
-    def stream(z, columns):
-        for i in range(19):
-            cx, cy, cz = VELOCITY[i]
-            source = z + 1 - cz
-            value = post[PLACE[i], source]
-            if cx:
-                a = SIGNS.index(cx)
-                line = xh[a, X_GROUP[a].index(i), source]
-                value = pltpu.roll(value, cx % rows, 0)
-                value = jnp.where(sub == (0 if cx == 1 else rows - 1), line, value)
-            if cy:
-                a = SIGNS.index(cy)
-                j = Y_GROUP[a].index(i)
-                value = pltpu.roll(value, cy % width, 1)
-                column = jnp.broadcast_to(
-                    columns[a][:, j * depth : j * depth + 1], (rows, width)
-                )
-                value = jnp.where(lane == (0 if cy == 1 else width - 1), column, value)
-            pre[i, z] = value
-        return tuple(pltpu.roll(c, width - 1, 1) for c in columns)
-
-    lax.fori_loop(0, depth, stream, tuple(columns), unroll=2)
+        column_out[a] = result
+    for a in range(2):
+        wrap = 0 if a == 0 else rows - 1
+        for k, i in enumerate(X_GROUP[a]):
+            cz = VELOCITY[i][2]
+            pre[PLACE[i], pl.ds((1 + cz) * rows + wrap, depth, stride=rows), :] = xh[a, k]
+            if cz:
+                first = (1 if cz == 1 else depth) * rows + wrap
+                pre[PLACE[i], first : first + 1, :] = xeh[a, SIGNS.index(cz), 0]
+    for a in range(2):
+        for j, i in enumerate(Y_GROUP[a]):
+            if VELOCITY[i][0]:
+                continue
+            at_edge = lane == (0 if a == 0 else width - 1)
+            for z in range(depth):
+                tile_rows = pl.ds((z + 1) * rows, rows)
+                place = j * depth + z
+                column = jnp.broadcast_to(columns[a][:, place : place + 1], (rows, width))
+                pre[PLACE[i], tile_rows] = jnp.where(at_edge, column, pre[PLACE[i], tile_rows])
 
     for copy in surfels:
         copy.wait()
@@ -489,32 +520,31 @@
 
     level_id = lax.broadcasted_iota(jnp.int32, (depth, n_surf), 0)
     for a in range(2):
-        other = theirs[a, CELL_ROW : CELL_ROW + 1, :].astype(jnp.int32)
+        other = theirs[a, CELL_ROW].astype(jnp.int32)
         pick = jnp.where(spot == lax.rem(other, width), 1.0, 0.0).astype(BF16)
         on_x = lax.rem(lax.div(other, width), rows) == (rows - 1 if a == 0 else 0)
         on_face = (level_id == lax.div(other, width * rows)) & on_x
         lines = jnp.concatenate(
-            [jnp.where(on_face, theirs[a, m : m + 1, :], 0.0) for m in range(MODES)], axis=0
+            [jnp.where(on_face, theirs[a, m], 0.0) for m in range(MODES)], axis=0
         )
         high, low = halves(lines)
         lines = dot_nt(high, pick) + dot_nt(low, pick)
-        density = xh[a, 5, pl.ds(1, depth)].reshape(depth, width)
+        density = xh[a, 5]
         for m in range(MODES):
             flux_x[a, m, 0:depth, :] = lines[m * depth : (m + 1) * depth] * density
         for b in range(2):
-            place, slot = (LOW, 0) if b == 0 else (HIGH, depth + 1)
-            line = xh[a, 5, slot]
+            place = LOW if b == 0 else HIGH
+            line = xeh[a, b, 1]
             for m in range(MODES):
                 flux_x[a, m, place : place + 1, :] = edges_in[a, b, m : m + 1, :] * line
         density = everywhere(yh[a], 5)
         for t in range(2):
             flux_y[a, t] = faces_in[a, t] * density
         for b in range(2):
-            density = everywhere(yxh[a, b], 5)
-            edge = rows - 1 if b == 0 else 0
+            density = everywhere(jnp.broadcast_to(yrh[a, b], (rows, width)), 5)
             for t in range(2):
                 k = 2 * a + b
-                flux_c[t, k : k + 1, :] = corners_in[a, b, t] * density[edge : edge + 1]
+                flux_c[t, k : k + 1, :] = corners_in[a, b, t] * density[0:1]
     flux_c[:, 4:, :] = jnp.zeros((2, rows - 4, width), F32)
     for a in range(2):
         for m in range(MODES):
@@ -524,13 +554,13 @@
 
 
 MOVED = X_GROUP[0] + X_GROUP[1]
-FIXED_RUNS = ((0, 1), (3, 4), (15, 4))
+FIXED_RUNS = ((0, 1), (3, 2), (5, 1), (6, 1), (15, 1), (16, 1), (17, 1), (18, 1))
 MOVED_RUNS = ((1, 2), (7, 8))
 N_CUTS = 4
 
 
-def apply(pre, flux_m, flux_x, flux_y, flux_c, total, drive, out, force_out, amp_out, stage, force, amplitude, sem):
-    depth, rows, width = pre.shape[1:]
+def apply(pre, flux_m, flux_x, flux_y, flux_c, column, total, drive, out, force_out, amp_out, stage, force, amplitude, sem):
+    depth, rows, width = flux_m.shape[1] - 2, flux_m.shape[2], flux_m.shape[3]
     copies = []
 
     def write(src, dst):
@@ -539,8 +569,8 @@
         copies.append(copy)
 
     for first, count in FIXED_RUNS:
-        run = pl.ds(first, count)
-        write(pre.at[run], out.at[run])
+        run = pl.ds(PLACE[first], count)
+        write(pre.at[run, pl.ds(rows, depth * rows)], out.at[pl.ds(first, count)])
 
     lane = lax.broadcasted_iota(jnp.int32, (rows, width), 1)
     sub = lax.broadcasted_iota(jnp.int32, (rows, width), 0)
@@ -575,7 +605,9 @@
         for b, t in enumerate(SIGNS):
             edge = corner[2 * a + b : 2 * a + b + 1]
             moved = pltpu.roll(face, t % rows, 0)
-            columns[t, s] = jnp.where(sub == (0 if t == 1 else rows - 1), edge, moved)
+            moved = jnp.where(sub == (0 if t == 1 else rows - 1), edge, moved)
+            i = VELOCITY.index((t, s, 0))
+            columns[t, s] = column[a] + COEF[i] * moved
 
     def weigh(terms):
         return tree_sum([amps[m] * terms[m] for m in range(MODES)])
@@ -587,9 +619,6 @@
         ]
         for a in range(2)
     ]
-
-    def put(i, z, value):
-        stage[i, z] = pre[i, z] + COEF[i] * value
 
     part = depth // N_CUTS
     for slot in range(depth + 2):
@@ -604,14 +633,16 @@
                 z = slot - 1 + cz
                 if not 0 <= z < depth:
                     continue
-                value = moved
+                value = pltpu.roll(moved, cy % width, 1) if cy else moved
+                value = pre[PLACE[i], (z + 1) * rows : (z + 2) * rows, :] + COEF[i] * value
                 if cy:
-                    value = pltpu.roll(moved, cy % width, 1)
-                    column = jnp.broadcast_to(columns[s, cy][:, z : z + 1], (rows, width))
-                    value = jnp.where(lane == (0 if cy == 1 else width - 1), column, value)
-                put(i, z, value)
+                    first = Y_GROUP[SIGNS.index(cy)].index(i) * depth + z
+                    beside = columns[s, cy][:, first : first + 1]
+                    beside = jnp.broadcast_to(beside, (rows, width))
+                    value = jnp.where(lane == (0 if cy == 1 else width - 1), beside, value)
+                stage[i, z * rows : (z + 1) * rows] = value
         if slot >= 2 and (slot - 1) % part == 0:
-            cut = pl.ds(slot - 1 - part, part)
+            cut = pl.ds((slot - 1 - part) * rows, part * rows)
             for first, count in MOVED_RUNS:
                 run = pl.ds(first, count)
                 write(stage.at[run, cut], out.at[run, cut])
@@ -633,16 +664,17 @@
     passed = pl.pallas_call(
         functools.partial(exchange, sizes),
         out_shape=(
-            jax.ShapeDtypeStruct(pops.shape, F32),
+            jax.ShapeDtypeStruct((19, (depth + 2) * rows, width), F32),
             jax.ShapeDtypeStruct((MODES, depth + 2) + tile, F32),
             jax.ShapeDtypeStruct((2, MODES, depth + rows, width), F32),
             jax.ShapeDtypeStruct((2, 2) + tile, F32),
+            jax.ShapeDtypeStruct((2,) + tile, F32),
             jax.ShapeDtypeStruct((2,) + tile, F32),
             jax.ShapeDtypeStruct((1, width), F32),
             jax.ShapeDtypeStruct((MODE_ROWS, PANELS), F32),
         ),
         in_specs=[hbm] * 8,
-        out_specs=(vmem,) * 7,
+        out_specs=(vmem,) * 8,
         scratch_shapes=[
             pltpu.VMEM(pops.shape, F32),
             pltpu.VMEM(solid.shape, jnp.int32),
@@ -652,17 +684,19 @@
             pltpu.VMEM((MODES, 1, n_surf), F32),
             pltpu.VMEM((1, PANELS), jnp.int32),
             pltpu.VMEM((1, MODES), F32),
-            pltpu.VMEM((MODE_ROWS, n_surf), F32),
+            pltpu.VMEM((MODES + 1, 1, n_surf), F32),
             dma((7 + N_LOADS,)),
-            pltpu.VMEM((19, depth + 2) + tile, F32),
-            pltpu.VMEM((depth,) + tile, F32),
-            pltpu.VMEM((2, 6, depth, 1, width), F32),
-            pltpu.VMEM((2, 6, depth + 2, 1, width), F32),
+            pltpu.VMEM((depth * rows, width), F32),
+            pltpu.VMEM((2, 6, depth, width), F32),
+            pltpu.VMEM((2, 6, depth, width), F32),
+            pltpu.VMEM((2, 2, 2, 1, width), F32),
+            pltpu.VMEM((2, 2, 2, 1, width), F32),
             pltpu.VMEM((2,) + tile, F32),
             pltpu.VMEM((2,) + tile, F32),
+            pltpu.VMEM((2, 2, 1, width), F32),
+            pltpu.VMEM((2, 2, 1, width), F32),
             pltpu.VMEM((2, 2) + tile, F32),
-            pltpu.VMEM((2, 2) + tile, F32),
-            pltpu.VMEM((2, MODE_ROWS, n_surf), F32),
+            pltpu.VMEM((2, MODES + 1, 1, n_surf), F32),
             pltpu.VMEM((2, 2, MODE_ROWS, width), F32),
             pltpu.VMEM((2, 2, MODE_ROWS, width), F32),
             pltpu.VMEM((2, 2) + tile, F32),
@@ -698,21 +732,21 @@
     read, force, amp = pl.pallas_call(
         apply,
         out_shape=(
-            jax.ShapeDtypeStruct(pops.shape, F32),
+            jax.ShapeDtypeStruct((19, depth * rows, width), F32),
             jax.ShapeDtypeStruct((1, PANELS), F32),
             jax.ShapeDtypeStruct((1, MODES), F32),
         ),
-        in_specs=[vmem] * 7,
+        in_specs=[vmem] * 8,
         out_specs=(hbm,) * 3,
         scratch_shapes=[
-            pltpu.VMEM(pops.shape, F32),
+            pltpu.VMEM((19, depth * rows, width), F32),
             pltpu.VMEM((1, PANELS), F32),
             pltpu.VMEM((1, MODES), F32),
             dma((len(FIXED_RUNS) + len(MOVED_RUNS) * N_CUTS + 2,)),
         ],
         compiler_params=pltpu.CompilerParams(vmem_limit_bytes=8 * 1024 * 1024),
     )(*passed)
-    return read, force.reshape(PANELS), amp.reshape(MODES)
+    return read.reshape(pops.shape), force.reshape(PANELS), amp.reshape(MODES)
 
 
 def solution(mesh):

time: 18.4 us -> 17.9 us (0.973)
  Pallas kernels: 17.6 us -> 17.1 us
    pallas_call x1, Pallas kernels: 16.2 us -> 15.6 us  [per_device(): pl.pallas_call(functools.partial(exchange, sizes), out_shape=(jax.ShapeDt...]
where the time goes in v2:
time: 17.9 us; the launch traced here: 17.7 us
  Pallas kernels  17.1 us (96%)
  between operations  0.64 us (4%)
    pallas_call x1, Pallas kernels, per_device(): pl.pallas_call(functools.partial(exchange, sizes), out_shape=(jax.ShapeDt...  15.6 us
    pallas_call x1, Pallas kernels, per_device(): pl.pallas_call(apply, out_shape=(jax.ShapeDtypeStruct((19, depth * rows,...  1.48 us

profile of v2, /device:TPU:0, one launch (start us, length us, event | category | flops | bytes accessed | tf_op | source)
XLA Modules:
  0.0 17.7 jit_solution(13210775088811200545)
XLA Ops:
  0.6 15.6 %shard_map.103 = (f32[19,144,128]{2,1,0:T(8,128)S(1)}, f32[12,18,8,128]{3,2,1,0:T(8,128)S(1)}, f32[2,12,24,128]{3,2,1,0:T(8,128)S(1)}, f32[2,2,8,128]{3,2,1,0:T(...) custom-call(f32[19,16,8,128]{3,2,1,0:T(8,128)} %pops_in.1, ...), custom_call_target="tpu_custom_call" | custom-call | tf_op jit(solution)/shard_map/pallas_call | solution.py:664
  16.2 1.5 %shard_map.104 = (f32[19,128,128]{2,1,0:T(8,128)}, f32[1,40]{1,0:T(1,128)}, f32[1,12]{1,0:T(1,128)}) custom-call(f32[19,144,128]{2,1,0:T(8,128)S(1)} %get-tuple-element.14.pre, f32[12,18,8,128]{3,2,1,0:T(8,128)S(1)} %get-tuple-element.15.flux_m, f32[2,12,24,128]{3,2,1,0:T(8,128)S(1)} %get-tuple-element.16.flux_x, ...), custom_call_target="tpu_custom_call" | custom-call | tf_op jit(solution)/shard_map/pallas_call | solution.py:732

commit v3 on v2

--- a/solution.py
+++ b/solution.py
@@ -102,7 +102,9 @@
     return terms[0]
 
 
-N_HALO = 18
+N_CHUNKS = 2
+UNROLL = 4
+N_HALO = 16 + 2 * N_CHUNKS
 PER_DOT = 2
 N_SURF = 2 + 4 + 2 + 4 + 2
 
@@ -149,7 +151,6 @@
     edges,
     edges_in,
     faces,
-    faces_in,
     corners,
     corners_in,
     surf_send,
@@ -205,23 +206,85 @@
     pick_col = jnp.where(spot == col, 1.0, 0.0).astype(BF16)
     on_row = lax.broadcasted_iota(jnp.int32, (cells, n_surf), 0) == row
 
-    table = [jnp.where(live, shape_rows[m] * WALL_SCALE, 0.0) for m in range(MODES)]
+    def add_up(z, carry):
+        density = pops[0, z]
+        for i in range(1, 19):
+            density = density + pops[i, z]
+        dens[pl.ds(pl.multiple_of(z * rows, rows), rows)] = density
+        return carry
+
+    for n in range(N_LOADS):
+        loads[len(small) + n].wait()
+        lax.fori_loop(n * part, (n + 1) * part, add_up, 0, unroll=True)
+    gauge_high, gauge_low = halves(dens[...] - 1.0)
+    by_row = dot(gauge_high, pick_col) + dot(gauge_low, pick_col)
+    excess = jnp.sum(jnp.where(on_row, by_row, 0.0), axis=0, keepdims=True)
+    contrib = jnp.where(live, area[...] * (excess / 3.0), 0.0)
+    pick_panel = jnp.where(spot == panel[...], 1.0, 0.0).astype(BF16)
+    contrib_high, contrib_low = halves(jnp.broadcast_to(contrib, (8, n_surf)))
+    partial = dot_nt(contrib_high, pick_panel) + dot_nt(contrib_low, pick_panel)
+    partial = partial[0:1]
+
+    pl.semaphore_wait(barrier, len(partners))
+
+    def stage_start(n, value):
+        stage = stages[n]
+        index = 0
+        for dim, axis in enumerate(AXES):
+            if axis in stage:
+                index = index * sizes[dim] + here[dim]
+        slots[n, index] = value
+        for offset in stage_offsets(stage, sizes):
+            pltpu.make_async_remote_copy(
+                src_ref=slots.at[n, index],
+                dst_ref=slots.at[n, index],
+                send_sem=stage_send.at[n],
+                recv_sem=stage_recv.at[n],
+                device_id=at(offset),
+                device_id_type=MESH,
+            ).start()
+
+    def stage_sum(n):
+        count = len(stage_offsets(stages[n], sizes))
+        whole = pltpu.make_async_remote_copy(
+            src_ref=slots.at[n, pl.ds(0, count)],
+            dst_ref=slots.at[n, pl.ds(0, count)],
+            send_sem=stage_send.at[n],
+            recv_sem=stage_recv.at[n],
+            device_id=at(stage_offsets(stages[n], sizes)[0]),
+            device_id_type=MESH,
+        )
+        whole.wait_recv()
+        whole.wait_send()
+        return tree_sum([slots[n, k] for k in range(count + 1)])
+
+    stage_start(0, partial)
+
+    surfels = []
+
+    def pass_on(src, dst, offset):
+        copy = pltpu.make_async_remote_copy(
+            src_ref=src,
+            dst_ref=dst,
+            send_sem=surf_send.at[len(surfels)],
+            recv_sem=surf_recv.at[len(surfels)],
+            device_id=at(offset),
+            device_id_type=MESH,
+        )
+        copy.start()
+        surfels.append(copy)
+
+    scale = WALL_SCALE * (excess + 1.0)
+    table = [jnp.where(live, shape_rows[m] * scale, 0.0) for m in range(MODES)]
     table.append(cell[...].astype(F32))
     for m, line in enumerate(table):
         mine[m] = line
     table = jnp.concatenate(
         table[:MODES] + [jnp.zeros((MODE_ROWS - MODES, n_surf), F32)], axis=0
     )
-    masked = []
-    for a in range(2):
-        on_x = cell_x == (rows - 1 if a == 0 else 0)
-        for b in range(2):
-            on_z = cell_z == (depth - 1 if b == 0 else 0)
-            masked.append(jnp.where(on_x & on_z, table, 0.0))
-    high, low = halves(jnp.concatenate(masked, axis=0))
-    edge_rows = dot_nt(high, pick_col) + dot_nt(low, pick_col)
-    for k in range(4):
-        edges[k // 2, k % 2] = edge_rows[k * MODE_ROWS : (k + 1) * MODE_ROWS]
+    for a, s in enumerate(SIGNS):
+        pass_on(mine, theirs.at[a], (s, 0, 0))
+
     row_id = lax.broadcasted_iota(jnp.int32, (rows, n_surf), 0)
     sides = jnp.concatenate(
         [
@@ -252,79 +315,9 @@
                 edge = a * rows + (rows - 1 if b == 0 else 0)
                 corners[a, b, t] = packed[edge : edge + 1]
 
-    def add_up(z, carry):
-        density = pops[0, z]
-        for i in range(1, 19):
-            density = density + pops[i, z]
-        dens[pl.ds(pl.multiple_of(z * rows, rows), rows)] = density
-        return carry
-
-    for n in range(N_LOADS):
-        loads[len(small) + n].wait()
-        lax.fori_loop(n * part, (n + 1) * part, add_up, 0, unroll=True)
-    gauge_high, gauge_low = halves(dens[...] - 1.0)
-    by_row = dot(gauge_high, pick_col) + dot(gauge_low, pick_col)
-    excess = jnp.sum(jnp.where(on_row, by_row, 0.0), axis=0, keepdims=True)
-    contrib = jnp.where(live, area[...] * (excess / 3.0), 0.0)
-    pick_panel = jnp.where(spot == panel[...], 1.0, 0.0).astype(BF16)
-    contrib_high, contrib_low = halves(jnp.broadcast_to(contrib, (8, n_surf)))
-    partial = dot_nt(contrib_high, pick_panel) + dot_nt(contrib_low, pick_panel)
-    partial = partial[0:1]
-
-    pl.semaphore_wait(barrier, len(partners))
-
-    def stage_start(n, value):
-        stage = stages[n]
-        index = 0
-        for dim, axis in enumerate(AXES):
-            if axis in stage:
-                index = index * sizes[dim] + here[dim]
-        slots[n, index] = value
-        for offset in stage_offsets(stage, sizes):
-            pltpu.make_async_remote_copy(
-                src_ref=slots.at[n, index],
-                dst_ref=slots.at[n, index],
-                send_sem=stage_send.at[n],
-                recv_sem=stage_recv.at[n],
-                device_id=at(offset),
-                device_id_type=MESH,
-            ).start()
-
-    def stage_sum(n):
-        count = len(stage_offsets(stages[n], sizes))
-        whole = pltpu.make_async_remote_copy(
-            src_ref=slots.at[n, pl.ds(0, count)],
-            dst_ref=slots.at[n, pl.ds(0, count)],
-            send_sem=stage_send.at[n],
-            recv_sem=stage_recv.at[n],
-            device_id=at(stage_offsets(stages[n], sizes)[0]),
-            device_id_type=MESH,
-        )
-        whole.wait_recv()
-        whole.wait_send()
-        return tree_sum([slots[n, k] for k in range(count + 1)])
-
-    stage_start(0, partial)
-
-    surfels = []
-
-    def pass_on(src, dst, offset):
-        copy = pltpu.make_async_remote_copy(
-            src_ref=src,
-            dst_ref=dst,
-            send_sem=surf_send.at[len(surfels)],
-            recv_sem=surf_recv.at[len(surfels)],
-            device_id=at(offset),
-            device_id_type=MESH,
-        )
-        copy.start()
-        surfels.append(copy)
-
     for a, s in enumerate(SIGNS):
-        pass_on(mine, theirs.at[a], (s, 0, 0))
-        pass_on(faces.at[a], faces_in.at[a], (0, s, 0))
+        pass_on(faces.at[a], flux_y.at[a], (0, s, 0))
         for b, t in enumerate(SIGNS):
-            pass_on(edges.at[a, b], edges_in.at[a, b], (s, 0, t))
             pass_on(corners.at[a, b], corners_in.at[a, b], (t, s, 0))
 
     loads[len(small) + N_LOADS].wait()
@@ -374,34 +367,7 @@
                 edge = 0 if cy == 1 else width - 1
                 pack(a, value, edge, Y_GROUP[a].index(i) * depth + place)
             pre[PLACE[i], pl.ds(pl.multiple_of((z + 1 + cz) * rows, rows), rows)] = value
-        for a in range(2):
-            pack(a, density, width - 1 if a == 0 else 0, 5 * depth + z)
         return tuple(packed)
-
-    zero = jnp.zeros((rows, width), F32)
-    packed = lax.fori_loop(0, depth, collide, (zero, zero))
-    line_lane = lax.broadcasted_iota(jnp.int32, (1, width), 1)
-    for a in range(2):
-        wrap, edge = (0, rows - 1) if a == 0 else (rows - 1, 0)
-        for k, i in enumerate(X_GROUP[a]):
-            cz = VELOCITY[i][2]
-            first = (1 + cz) * rows + wrap
-            xs[a, k] = pre[PLACE[i], pl.ds(first, depth, stride=rows), :]
-            if cz:
-                b = SIGNS.index(cz)
-                first = (depth + 1 if b == 0 else 0) * rows + wrap
-                xe[a, b, 0] = pre[PLACE[i], first : first + 1, :]
-        xs[a, 5] = dens[pl.ds(edge, depth, stride=rows), :]
-        for b in range(2):
-            first = (depth - 1 if b == 0 else 0) * rows + edge
-            xe[a, b, 1] = dens[first : first + 1, :]
-            wrap_b, edge_b = (0, rows - 1) if b == 0 else (rows - 1, 0)
-            yr[a, b] = jnp.where(
-                line_lane < 5 * depth,
-                packed[a][wrap_b : wrap_b + 1],
-                packed[a][edge_b : edge_b + 1],
-            )
-        ys[a] = packed[a]
 
     halo = []
 
@@ -417,8 +383,31 @@
         copy.start()
         halo.append(copy)
 
+    zero = jnp.zeros((rows, width), F32)
+    packed = (zero, zero)
+    chunk = depth // N_CHUNKS
+    for n in range(N_CHUNKS):
+        packed = lax.fori_loop(n * chunk, (n + 1) * chunk, collide, packed, unroll=UNROLL)
+        for a, s in enumerate(SIGNS):
+            wrap = 0 if a == 0 else rows - 1
+            for k, i in enumerate(X_GROUP[a]):
+                first = (n * chunk + 1 + VELOCITY[i][2]) * rows + wrap
+                xs[a, n, k] = pre[PLACE[i], pl.ds(first, chunk, stride=rows), :]
+            send(xs.at[a, n], xh.at[a, n], (s, 0, 0))
+    for a in range(2):
+        wrap = 0 if a == 0 else rows - 1
+        for k, i in enumerate(X_GROUP[a]):
+            cz = VELOCITY[i][2]
+            if cz:
+                b = SIGNS.index(cz)
+                first = (depth + 1 if b == 0 else 0) * rows + wrap
+                xe[a, b] = pre[PLACE[i], first : first + 1, :]
+        for b in range(2):
+            wrap = 0 if b == 0 else rows - 1
+            yr[a, b] = packed[a][wrap : wrap + 1]
+        ys[a] = packed[a]
+
     for a, s in enumerate(SIGNS):
-        send(xs.at[a], xh.at[a], (s, 0, 0))
         send(ys.at[a], yh.at[a], (0, s, 0))
         for b, t in enumerate(SIGNS):
             send(yr.at[a, b], yrh.at[a, b], (t, s, 0))
@@ -449,12 +438,11 @@
             first = 2 * k * half
             flux = found[first : first + half] + found[first + half : first + 2 * half]
             for h in range(2):
-                value = flux[:, h * width : (h + 1) * width] * dens[h * half : (h + 1) * half]
-                value = value.reshape(depth // 2, rows, width)
+                value = flux[:, h * width : (h + 1) * width].reshape(depth // 2, rows, width)
                 flux_m[step * PER_DOT + k, pl.ds(1 + h * (depth // 2), depth // 2)] = value
         return carry
 
-    lax.fori_loop(0, MODES // PER_DOT, scatter, 0)
+    lax.fori_loop(0, MODES // PER_DOT, scatter, 0, unroll=True)
     for a, s in enumerate(SIGNS):
         source, target = (depth, 0) if a == 0 else (1, depth + 1)
         pass_on(flux_m.at[:, source], flux_m.at[:, target], (0, 0, s))
@@ -470,6 +458,34 @@
 
     for n in range(1, len(stages)):
         stage_start(n, stage_sum(n - 1))
+
+    for copy in surfels[:-2]:
+        copy.wait()
+    late = len(surfels) - 2
+    level_id = lax.broadcasted_iota(jnp.int32, (depth, n_surf), 0)
+    for a in range(2):
+        other = theirs[a, CELL_ROW].astype(jnp.int32)
+        pick = jnp.where(spot == lax.rem(other, width), 1.0, 0.0).astype(BF16)
+        on_x = lax.rem(lax.div(other, width), rows) == (rows - 1 if a == 0 else 0)
+        on_face = (level_id == lax.div(other, width * rows)) & on_x
+        lines = jnp.concatenate(
+            [jnp.where(on_face, theirs[a, m], 0.0) for m in range(MODES)], axis=0
+        )
+        high, low = halves(lines)
+        lines = dot_nt(high, pick) + dot_nt(low, pick)
+        for m in range(MODES):
+            flux_x[a, m, 0:depth, :] = lines[m * depth : (m + 1) * depth]
+            flux_x[a, m, HIGH + 1 :, :] = jnp.zeros((rows - 2, width), F32)
+            for b in range(2):
+                first = m * depth + (depth - 1 if b == 0 else 0)
+                edges[a, b, m : m + 1, :] = lines[first : first + 1]
+        for b, t in enumerate(SIGNS):
+            edges[a, b, MODES:, :] = jnp.zeros((MODE_ROWS - MODES, width), F32)
+            pass_on(edges.at[a, b], edges_in.at[a, b], (0, 0, t))
+            for t in range(2):
+                k = 2 * a + b
+                flux_c[t, k : k + 1, :] = corners_in[a, b, t]
+    flux_c[:, 4:, :] = jnp.zeros((2, rows - 4, width), F32)
 
     for copy in halo:
         copy.wait()
@@ -492,10 +508,12 @@
         wrap = 0 if a == 0 else rows - 1
         for k, i in enumerate(X_GROUP[a]):
             cz = VELOCITY[i][2]
-            pre[PLACE[i], pl.ds((1 + cz) * rows + wrap, depth, stride=rows), :] = xh[a, k]
+            for n in range(N_CHUNKS):
+                first = (n * chunk + 1 + cz) * rows + wrap
+                pre[PLACE[i], pl.ds(first, chunk, stride=rows), :] = xh[a, n, k]
             if cz:
                 first = (1 if cz == 1 else depth) * rows + wrap
-                pre[PLACE[i], first : first + 1, :] = xeh[a, SIGNS.index(cz), 0]
+                pre[PLACE[i], first : first + 1, :] = xeh[a, SIGNS.index(cz)]
     for a in range(2):
         for j, i in enumerate(Y_GROUP[a]):
             if VELOCITY[i][0]:
@@ -507,48 +525,14 @@
                 column = jnp.broadcast_to(columns[a][:, place : place + 1], (rows, width))
                 pre[PLACE[i], tile_rows] = jnp.where(at_edge, column, pre[PLACE[i], tile_rows])
 
-    for copy in surfels:
+
+    for copy in surfels[late:]:
         copy.wait()
-
-    def everywhere(tile, group):
-        tile = jnp.where(lane // depth == group, tile, 0.0)
-        step = depth
-        while step < width:
-            tile = tile + pltpu.roll(tile, step, 1)
-            step *= 2
-        return tile
-
-    level_id = lax.broadcasted_iota(jnp.int32, (depth, n_surf), 0)
     for a in range(2):
-        other = theirs[a, CELL_ROW].astype(jnp.int32)
-        pick = jnp.where(spot == lax.rem(other, width), 1.0, 0.0).astype(BF16)
-        on_x = lax.rem(lax.div(other, width), rows) == (rows - 1 if a == 0 else 0)
-        on_face = (level_id == lax.div(other, width * rows)) & on_x
-        lines = jnp.concatenate(
-            [jnp.where(on_face, theirs[a, m], 0.0) for m in range(MODES)], axis=0
-        )
-        high, low = halves(lines)
-        lines = dot_nt(high, pick) + dot_nt(low, pick)
-        density = xh[a, 5]
-        for m in range(MODES):
-            flux_x[a, m, 0:depth, :] = lines[m * depth : (m + 1) * depth] * density
         for b in range(2):
             place = LOW if b == 0 else HIGH
-            line = xeh[a, b, 1]
             for m in range(MODES):
-                flux_x[a, m, place : place + 1, :] = edges_in[a, b, m : m + 1, :] * line
-        density = everywhere(yh[a], 5)
-        for t in range(2):
-            flux_y[a, t] = faces_in[a, t] * density
-        for b in range(2):
-            density = everywhere(jnp.broadcast_to(yrh[a, b], (rows, width)), 5)
-            for t in range(2):
-                k = 2 * a + b
-                flux_c[t, k : k + 1, :] = corners_in[a, b, t] * density[0:1]
-    flux_c[:, 4:, :] = jnp.zeros((2, rows - 4, width), F32)
-    for a in range(2):
-        for m in range(MODES):
-            flux_x[a, m, HIGH + 1 :, :] = jnp.zeros((rows - 2, width), F32)
+                flux_x[a, m, place : place + 1, :] = edges_in[a, b, m : m + 1, :]
 
     total_out[...] = stage_sum(len(stages) - 1)
 
@@ -687,10 +671,10 @@
             pltpu.VMEM((MODES + 1, 1, n_surf), F32),
             dma((7 + N_LOADS,)),
             pltpu.VMEM((depth * rows, width), F32),
-            pltpu.VMEM((2, 6, depth, width), F32),
-            pltpu.VMEM((2, 6, depth, width), F32),
-            pltpu.VMEM((2, 2, 2, 1, width), F32),
-            pltpu.VMEM((2, 2, 2, 1, width), F32),
+            pltpu.VMEM((2, N_CHUNKS, 5, depth // N_CHUNKS, width), F32),
+            pltpu.VMEM((2, N_CHUNKS, 5, depth // N_CHUNKS, width), F32),
+            pltpu.VMEM((2, 2, 1, width), F32),
+            pltpu.VMEM((2, 2, 1, width), F32),
             pltpu.VMEM((2,) + tile, F32),
             pltpu.VMEM((2,) + tile, F32),
             pltpu.VMEM((2, 2, 1, width), F32),
@@ -699,7 +683,6 @@
             pltpu.VMEM((2, MODES + 1, 1, n_surf), F32),
             pltpu.VMEM((2, 2, MODE_ROWS, width), F32),
             pltpu.VMEM((2, 2, MODE_ROWS, width), F32),
-            pltpu.VMEM((2, 2) + tile, F32),
             pltpu.VMEM((2, 2) + tile, F32),
             pltpu.VMEM((2, 2, 2, 1, width), F32),
             pltpu.VMEM((2, 2, 2, 1, width), F32),

time: 17.9 us -> 15.7 us (0.88)
  Pallas kernels: 17.1 us -> 14.9 us
    pallas_call x1, Pallas kernels: 15.6 us -> 13.4 us  [per_device(): pl.pallas_call(functools.partial(exchange, sizes), out_shape=(jax.ShapeDt...]
where the time goes in v3:
time: 15.7 us; the launch traced here: 15.6 us
  Pallas kernels  14.9 us (95%)
  between operations  0.64 us (4%)
    pallas_call x1, Pallas kernels, per_device(): pl.pallas_call(functools.partial(exchange, sizes), out_shape=(jax.ShapeDt...  13.4 us
    pallas_call x1, Pallas kernels, per_device(): pl.pallas_call(apply, out_shape=(jax.ShapeDtypeStruct((19, depth * rows,...  1.48 us

profile of v3, /device:TPU:0, one launch (start us, length us, event | category | flops | bytes accessed | tf_op | source)
XLA Modules:
  0.0 15.6 jit_solution(17527921695417275595)
XLA Ops:
  0.6 13.4 %shard_map.103 = (f32[19,144,128]{2,1,0:T(8,128)S(1)}, f32[12,18,8,128]{3,2,1,0:T(8,128)S(1)}, f32[2,12,24,128]{3,2,1,0:T(8,128)S(1)}, f32[2,2,8,128]{3,2,1,0:T(...) custom-call(f32[19,16,8,128]{3,2,1,0:T(8,128)} %pops_in.1, ...), custom_call_target="tpu_custom_call" | custom-call | tf_op jit(solution)/shard_map/pallas_call | solution.py:648
  14.1 1.5 %shard_map.104 = (f32[19,128,128]{2,1,0:T(8,128)}, f32[1,40]{1,0:T(1,128)}, f32[1,12]{1,0:T(1,128)}) custom-call(f32[19,144,128]{2,1,0:T(8,128)S(1)} %get-tuple-element.14.pre, f32[12,18,8,128]{3,2,1,0:T(8,128)S(1)} %get-tuple-element.15.flux_m, f32[2,12,24,128]{3,2,1,0:T(8,128)S(1)} %get-tuple-element.16.flux_x, ...), custom_call_target="tpu_custom_call" | custom-call | tf_op jit(solution)/shard_map/pallas_call | solution.py:715

commit v4 on v3

--- a/solution.py
+++ b/solution.py
@@ -102,9 +102,8 @@
     return terms[0]
 
 
-N_CHUNKS = 2
 UNROLL = 4
-N_HALO = 16 + 2 * N_CHUNKS
+N_HALO = 18
 PER_DOT = 2
 N_SURF = 2 + 4 + 2 + 4 + 2
 
@@ -137,6 +136,7 @@
     compliance,
     mine,
     load_sem,
+    post,
     dens,
     xs,
     xh,
@@ -216,17 +216,6 @@
     for n in range(N_LOADS):
         loads[len(small) + n].wait()
         lax.fori_loop(n * part, (n + 1) * part, add_up, 0, unroll=True)
-    gauge_high, gauge_low = halves(dens[...] - 1.0)
-    by_row = dot(gauge_high, pick_col) + dot(gauge_low, pick_col)
-    excess = jnp.sum(jnp.where(on_row, by_row, 0.0), axis=0, keepdims=True)
-    contrib = jnp.where(live, area[...] * (excess / 3.0), 0.0)
-    pick_panel = jnp.where(spot == panel[...], 1.0, 0.0).astype(BF16)
-    contrib_high, contrib_low = halves(jnp.broadcast_to(contrib, (8, n_surf)))
-    partial = dot_nt(contrib_high, pick_panel) + dot_nt(contrib_low, pick_panel)
-    partial = partial[0:1]
-
-    pl.semaphore_wait(barrier, len(partners))
-
     def stage_start(n, value):
         stage = stages[n]
         index = 0
@@ -258,8 +247,6 @@
         whole.wait_send()
         return tree_sum([slots[n, k] for k in range(count + 1)])
 
-    stage_start(0, partial)
-
     surfels = []
 
     def pass_on(src, dst, offset):
@@ -274,6 +261,16 @@
         copy.start()
         surfels.append(copy)
 
+    gauge_high, gauge_low = halves(dens[...] - 1.0)
+    by_row = dot(gauge_high, pick_col) + dot(gauge_low, pick_col)
+    excess = jnp.sum(jnp.where(on_row, by_row, 0.0), axis=0, keepdims=True)
+    contrib = jnp.where(live, area[...] * (excess / 3.0), 0.0)
+    pick_panel = jnp.where(spot == panel[...], 1.0, 0.0).astype(BF16)
+    contrib_high, contrib_low = halves(jnp.broadcast_to(contrib, (8, n_surf)))
+    partial = dot_nt(contrib_high, pick_panel) + dot_nt(contrib_low, pick_panel)
+    partial = partial[0:1]
+
+
     scale = WALL_SCALE * (excess + 1.0)
     table = [jnp.where(live, shape_rows[m] * scale, 0.0) for m in range(MODES)]
     table.append(cell[...].astype(F32))
@@ -282,43 +279,16 @@
     table = jnp.concatenate(
         table[:MODES] + [jnp.zeros((MODE_ROWS - MODES, n_surf), F32)], axis=0
     )
+
+    pl.semaphore_wait(barrier, len(partners))
+
+
     for a, s in enumerate(SIGNS):
         pass_on(mine, theirs.at[a], (s, 0, 0))
 
-    row_id = lax.broadcasted_iota(jnp.int32, (rows, n_surf), 0)
-    sides = jnp.concatenate(
-        [
-            jnp.where((row_id == cell_x) & (col == (width - 1 if a == 0 else 0)), 1.0, 0.0)
-            for a in range(2)
-        ],
-        axis=0,
-    ).astype(BF16)
-    on_z = lax.rem(spot, depth) == cell_z
-    for t in range(2):
-        spread_rows = jnp.concatenate(
-            [
-                jnp.broadcast_to(
-                    table[t * groups + g : t * groups + g + 1, :]
-                    if t * groups + g < MODES
-                    else jnp.zeros((1, n_surf), F32),
-                    (depth, n_surf),
-                )
-                for g in range(groups)
-            ],
-            axis=0,
-        )
-        high, low = halves(jnp.where(on_z, spread_rows, 0.0))
-        packed = dot_nt(sides, high) + dot_nt(sides, low)
-        for a in range(2):
-            faces[a, t] = packed[a * rows : (a + 1) * rows]
-            for b in range(2):
-                edge = a * rows + (rows - 1 if b == 0 else 0)
-                corners[a, b, t] = packed[edge : edge + 1]
-
-    for a, s in enumerate(SIGNS):
-        pass_on(faces.at[a], flux_y.at[a], (0, s, 0))
-        for b, t in enumerate(SIGNS):
-            pass_on(corners.at[a, b], corners_in.at[a, b], (t, s, 0))
+
+    stage_start(0, partial)
+
 
     loads[len(small) + N_LOADS].wait()
 
@@ -357,16 +327,16 @@
 
         for i in range(19):
             cx, cy, cz = VELOCITY[i]
-            value = new[i]
-            if cx:
-                value = pltpu.roll(value, cx % rows, 0)
+            if cx or cy:
+                post[PLACE[i], pl.ds(pl.multiple_of(z * rows, rows), rows)] = new[i]
+            else:
+                slot = pl.multiple_of((z + 1 + cz) * rows, rows)
+                pre[PLACE[i], pl.ds(slot, rows)] = new[i]
             if cy:
-                value = pltpu.roll(value, cy % width, 1)
                 a = SIGNS.index(cy)
                 place = z if cz == 0 else lax.rem(z + cz + depth, depth)
-                edge = 0 if cy == 1 else width - 1
-                pack(a, value, edge, Y_GROUP[a].index(i) * depth + place)
-            pre[PLACE[i], pl.ds(pl.multiple_of((z + 1 + cz) * rows, rows), rows)] = value
+                edge = width - 1 if cy == 1 else 0
+                pack(a, new[i], edge, Y_GROUP[a].index(i) * depth + place)
         return tuple(packed)
 
     halo = []
@@ -383,29 +353,44 @@
         copy.start()
         halo.append(copy)
 
+    def shift(i, value):
+        cx, cy, _ = VELOCITY[i]
+        if cx:
+            value = pltpu.roll(value, cx % rows, 0)
+        if cy:
+            value = pltpu.roll(value, cy % width, 1)
+        return value
+
     zero = jnp.zeros((rows, width), F32)
-    packed = (zero, zero)
-    chunk = depth // N_CHUNKS
-    for n in range(N_CHUNKS):
-        packed = lax.fori_loop(n * chunk, (n + 1) * chunk, collide, packed, unroll=UNROLL)
-        for a, s in enumerate(SIGNS):
-            wrap = 0 if a == 0 else rows - 1
-            for k, i in enumerate(X_GROUP[a]):
-                first = (n * chunk + 1 + VELOCITY[i][2]) * rows + wrap
-                xs[a, n, k] = pre[PLACE[i], pl.ds(first, chunk, stride=rows), :]
-            send(xs.at[a, n], xh.at[a, n], (s, 0, 0))
-    for a in range(2):
-        wrap = 0 if a == 0 else rows - 1
+    packed = lax.fori_loop(0, depth, collide, (zero, zero), unroll=UNROLL)
+    for a, s in enumerate(SIGNS):
+        edge = rows - 1 if a == 0 else 0
         for k, i in enumerate(X_GROUP[a]):
-            cz = VELOCITY[i][2]
+            _, cy, cz = VELOCITY[i]
+            line = post[PLACE[i], pl.ds(edge, depth, stride=rows), :]
+            if cy:
+                line = pltpu.roll(line, cy % width, 1)
+            xs[a, k] = line
             if cz:
-                b = SIGNS.index(cz)
-                first = (depth + 1 if b == 0 else 0) * rows + wrap
-                xe[a, b] = pre[PLACE[i], first : first + 1, :]
+                place = depth - 1 if cz == 1 else 0
+                xe[a, SIGNS.index(cz)] = line[place : place + 1]
+        send(xs.at[a], xh.at[a], (s, 0, 0))
+    for a, s in enumerate(SIGNS):
+        z, source, target = (depth - 1, depth + 1, 1) if a == 0 else (0, 0, depth)
+        for i in Z_GROUP[a]:
+            if VELOCITY[i][0] or VELOCITY[i][1]:
+                value = shift(i, post[PLACE[i], z * rows : (z + 1) * rows, :])
+                pre[PLACE[i], source * rows : (source + 1) * rows, :] = value
+        tile = packed[a]
+        for j, i in enumerate(Y_GROUP[a]):
+            cx = VELOCITY[i][0]
+            if cx:
+                own = (lane >= j * depth) & (lane < (j + 1) * depth)
+                tile = jnp.where(own, pltpu.roll(packed[a], cx % rows, 0), tile)
+        ys[a] = tile
         for b in range(2):
             wrap = 0 if b == 0 else rows - 1
-            yr[a, b] = packed[a][wrap : wrap + 1]
-        ys[a] = packed[a]
+            yr[a, b] = tile[wrap : wrap + 1]
 
     for a, s in enumerate(SIGNS):
         send(ys.at[a], yh.at[a], (0, s, 0))
@@ -420,6 +405,58 @@
             pre.at[group, pl.ds(target * rows, rows)],
             (0, 0, s),
         )
+
+
+    masked = []
+    for a in range(2):
+        on_x = cell_x == (rows - 1 if a == 0 else 0)
+        for b in range(2):
+            on_level = cell_z == (depth - 1 if b == 0 else 0)
+            masked.append(jnp.where(on_x & on_level, table, 0.0))
+    high, low = halves(jnp.concatenate(masked, axis=0))
+    edge_rows = dot_nt(high, pick_col) + dot_nt(low, pick_col)
+    for a, s in enumerate(SIGNS):
+        for b, t in enumerate(SIGNS):
+            first = (2 * a + b) * MODE_ROWS
+            edges[a, b] = edge_rows[first : first + MODE_ROWS]
+            pass_on(edges.at[a, b], edges_in.at[a, b], (s, 0, t))
+
+
+    row_id = lax.broadcasted_iota(jnp.int32, (rows, n_surf), 0)
+    sides = jnp.concatenate(
+        [
+            jnp.where((row_id == cell_x) & (col == (width - 1 if a == 0 else 0)), 1.0, 0.0)
+            for a in range(2)
+        ],
+        axis=0,
+    ).astype(BF16)
+    on_z = lax.rem(spot, depth) == cell_z
+    for t in range(2):
+        spread_rows = jnp.concatenate(
+            [
+                jnp.broadcast_to(
+                    table[t * groups + g : t * groups + g + 1, :]
+                    if t * groups + g < MODES
+                    else jnp.zeros((1, n_surf), F32),
+                    (depth, n_surf),
+                )
+                for g in range(groups)
+            ],
+            axis=0,
+        )
+        high, low = halves(jnp.where(on_z, spread_rows, 0.0))
+        shared = dot_nt(sides, high) + dot_nt(sides, low)
+        for a in range(2):
+            faces[a, t] = shared[a * rows : (a + 1) * rows]
+            for b in range(2):
+                edge = a * rows + (rows - 1 if b == 0 else 0)
+                corners[a, b, t] = shared[edge : edge + 1]
+
+    for a, s in enumerate(SIGNS):
+        pass_on(faces.at[a], flux_y.at[a], (0, s, 0))
+        for b, t in enumerate(SIGNS):
+            pass_on(corners.at[a, b], corners_in.at[a, b], (t, s, 0))
+
 
     half = cells // 2
     in_row = lax.broadcasted_iota(jnp.int32, (half, n_surf), 0) == lax.rem(row, half)
@@ -447,6 +484,14 @@
         source, target = (depth, 0) if a == 0 else (1, depth + 1)
         pass_on(flux_m.at[:, source], flux_m.at[:, target], (0, 0, s))
 
+    for z in range(depth):
+        for i in range(19):
+            cx, cy, cz = VELOCITY[i]
+            if (cx or cy) and 0 <= z + cz < depth:
+                slot = (z + 1 + cz) * rows
+                value = shift(i, post[PLACE[i], z * rows : (z + 1) * rows, :])
+                pre[PLACE[i], slot : slot + rows, :] = value
+
     for copy in loads[len(small) + N_LOADS + 1 :]:
         copy.wait()
     mode_id = lax.broadcasted_iota(jnp.int32, (MODE_ROWS, PANELS), 0)
@@ -459,9 +504,8 @@
     for n in range(1, len(stages)):
         stage_start(n, stage_sum(n - 1))
 
-    for copy in surfels[:-2]:
+    for copy in surfels[:2]:
         copy.wait()
-    late = len(surfels) - 2
     level_id = lax.broadcasted_iota(jnp.int32, (depth, n_surf), 0)
     for a in range(2):
         other = theirs[a, CELL_ROW].astype(jnp.int32)
@@ -476,15 +520,6 @@
         for m in range(MODES):
             flux_x[a, m, 0:depth, :] = lines[m * depth : (m + 1) * depth]
             flux_x[a, m, HIGH + 1 :, :] = jnp.zeros((rows - 2, width), F32)
-            for b in range(2):
-                first = m * depth + (depth - 1 if b == 0 else 0)
-                edges[a, b, m : m + 1, :] = lines[first : first + 1]
-        for b, t in enumerate(SIGNS):
-            edges[a, b, MODES:, :] = jnp.zeros((MODE_ROWS - MODES, width), F32)
-            pass_on(edges.at[a, b], edges_in.at[a, b], (0, 0, t))
-            for t in range(2):
-                k = 2 * a + b
-                flux_c[t, k : k + 1, :] = corners_in[a, b, t]
     flux_c[:, 4:, :] = jnp.zeros((2, rows - 4, width), F32)
 
     for copy in halo:
@@ -508,9 +543,8 @@
         wrap = 0 if a == 0 else rows - 1
         for k, i in enumerate(X_GROUP[a]):
             cz = VELOCITY[i][2]
-            for n in range(N_CHUNKS):
-                first = (n * chunk + 1 + cz) * rows + wrap
-                pre[PLACE[i], pl.ds(first, chunk, stride=rows), :] = xh[a, n, k]
+            first = (1 + cz) * rows + wrap
+            pre[PLACE[i], pl.ds(first, depth, stride=rows), :] = xh[a, k]
             if cz:
                 first = (1 if cz == 1 else depth) * rows + wrap
                 pre[PLACE[i], first : first + 1, :] = xeh[a, SIGNS.index(cz)]
@@ -526,13 +560,16 @@
                 pre[PLACE[i], tile_rows] = jnp.where(at_edge, column, pre[PLACE[i], tile_rows])
 
 
-    for copy in surfels[late:]:
+    for copy in surfels[2:]:
         copy.wait()
     for a in range(2):
         for b in range(2):
             place = LOW if b == 0 else HIGH
             for m in range(MODES):
                 flux_x[a, m, place : place + 1, :] = edges_in[a, b, m : m + 1, :]
+            for t in range(2):
+                k = 2 * a + b
+                flux_c[t, k : k + 1, :] = corners_in[a, b, t]
 
     total_out[...] = stage_sum(len(stages) - 1)
 
@@ -670,9 +707,10 @@
             pltpu.VMEM((1, MODES), F32),
             pltpu.VMEM((MODES + 1, 1, n_surf), F32),
             dma((7 + N_LOADS,)),
+            pltpu.VMEM((19, depth * rows, width), F32),
             pltpu.VMEM((depth * rows, width), F32),
-            pltpu.VMEM((2, N_CHUNKS, 5, depth // N_CHUNKS, width), F32),
-            pltpu.VMEM((2, N_CHUNKS, 5, depth // N_CHUNKS, width), F32),
+            pltpu.VMEM((2, 5, depth, width), F32),
+            pltpu.VMEM((2, 5, depth, width), F32),
             pltpu.VMEM((2, 2, 1, width), F32),
             pltpu.VMEM((2, 2, 1, width), F32),
             pltpu.VMEM((2,) + tile, F32),

time: 15.7 us -> 15.5 us (0.987)
  Pallas kernels: 14.9 us -> 14.7 us
    pallas_call x1, Pallas kernels: 13.4 us -> 13.2 us  [per_device(): pl.pallas_call(functools.partial(exchange, sizes), out_shape=(jax.ShapeDt...]
where the time goes in v4:
time: 15.5 us; the launch traced here: 15.4 us
  Pallas kernels  14.7 us (95%)
  between operations  0.64 us (4%)
    pallas_call x1, Pallas kernels, per_device(): pl.pallas_call(functools.partial(exchange, sizes), out_shape=(jax.ShapeDt...  13.2 us
    pallas_call x1, Pallas kernels, per_device(): pl.pallas_call(apply, out_shape=(jax.ShapeDtypeStruct((19, depth * rows,...  1.48 us

profile of v4, /device:TPU:0, one launch (start us, length us, event | category | flops | bytes accessed | tf_op | source)
XLA Modules:
  0.0 15.4 jit_solution(17283010202296943477)
XLA Ops:
  0.6 13.2 %shard_map.103 = (f32[19,144,128]{2,1,0:T(8,128)S(1)}, f32[12,18,8,128]{3,2,1,0:T(8,128)S(1)}, f32[2,12,24,128]{3,2,1,0:T(8,128)S(1)}, f32[2,2,8,128]{3,2,1,0:T(...) custom-call(f32[19,16,8,128]{3,2,1,0:T(8,128)} %pops_in.1, ...), custom_call_target="tpu_custom_call" | custom-call | tf_op jit(solution)/shard_map/pallas_call | solution.py:685
  13.9 1.5 %shard_map.104 = (f32[19,128,128]{2,1,0:T(8,128)}, f32[1,40]{1,0:T(1,128)}, f32[1,12]{1,0:T(1,128)}) custom-call(f32[19,144,128]{2,1,0:T(8,128)S(1)} %get-tuple-element.14.pre, f32[12,18,8,128]{3,2,1,0:T(8,128)S(1)} %get-tuple-element.15.flux_m, f32[2,12,24,128]{3,2,1,0:T(8,128)S(1)} %get-tuple-element.16.flux_x, ...), custom_call_target="tpu_custom_call" | custom-call | tf_op jit(solution)/shard_map/pallas_call | solution.py:753

commit v5 on v4

--- a/solution.py
+++ b/solution.py
@@ -48,7 +48,7 @@
 PLACE = tuple(ORDER.index(i) for i in range(19))
 AXES = ("gx", "gy", "gz")
 MESH = pl.DeviceIdType.MESH
-N_LOADS = 4
+N_LOADS = 2
 MODE_ROWS = 16
 CELL_ROW = MODES
 LOW, HIGH = 16, 17
@@ -182,9 +182,9 @@
         pl.semaphore_signal(barrier, inc=1, device_id=at(offset), device_id_type=MESH)
 
     small = [(cell_in, cell), (panel_in, panel), (area_in, area), (shapes_in, shape_rows)]
-    part = depth // N_LOADS
-    cuts = [pl.ds(n * part, part) for n in range(N_LOADS)]
-    big = [(pops_in.at[:, c], pops.at[:, c]) for c in cuts]
+    starts = [19 * n // N_LOADS for n in range(N_LOADS + 1)]
+    cuts = [pl.ds(a, b - a) for a, b in zip(starts[:-1], starts[1:])]
+    big = [(pops_in.at[c], pops.at[c]) for c in cuts]
     late = [(solid_in, solid), (panel_mode_in, panel_mode), (compliance_in, compliance)]
     loads = []
     for n, (src, dst) in enumerate(small + big + late):
@@ -206,16 +206,12 @@
     pick_col = jnp.where(spot == col, 1.0, 0.0).astype(BF16)
     on_row = lax.broadcasted_iota(jnp.int32, (cells, n_surf), 0) == row
 
-    def add_up(z, carry):
-        density = pops[0, z]
-        for i in range(1, 19):
-            density = density + pops[i, z]
-        dens[pl.ds(pl.multiple_of(z * rows, rows), rows)] = density
-        return carry
-
     for n in range(N_LOADS):
         loads[len(small) + n].wait()
-        lax.fori_loop(n * part, (n + 1) * part, add_up, 0, unroll=True)
+        for z in range(depth):
+            place = slice(z * rows, (z + 1) * rows)
+            density = tree_sum([pops[i, z] for i in range(starts[n], starts[n + 1])])
+            dens[place, :] = density if n == 0 else dens[place, :] + density
     def stage_start(n, value):
         stage = stages[n]
         index = 0
@@ -418,7 +414,8 @@
     for a, s in enumerate(SIGNS):
         for b, t in enumerate(SIGNS):
             first = (2 * a + b) * MODE_ROWS
-            edges[a, b] = edge_rows[first : first + MODE_ROWS]
+            for m in range(MODES):
+                edges[a, b, m] = edge_rows[first + m : first + m + 1]
             pass_on(edges.at[a, b], edges_in.at[a, b], (s, 0, t))
 
 
@@ -566,7 +563,7 @@
         for b in range(2):
             place = LOW if b == 0 else HIGH
             for m in range(MODES):
-                flux_x[a, m, place : place + 1, :] = edges_in[a, b, m : m + 1, :]
+                flux_x[a, m, place : place + 1, :] = edges_in[a, b, m]
             for t in range(2):
                 k = 2 * a + b
                 flux_c[t, k : k + 1, :] = corners_in[a, b, t]
@@ -719,8 +716,8 @@
             pltpu.VMEM((2, 2, 1, width), F32),
             pltpu.VMEM((2, 2) + tile, F32),
             pltpu.VMEM((2, MODES + 1, 1, n_surf), F32),
-            pltpu.VMEM((2, 2, MODE_ROWS, width), F32),
-            pltpu.VMEM((2, 2, MODE_ROWS, width), F32),
+            pltpu.VMEM((2, 2, MODES, 1, width), F32),
+            pltpu.VMEM((2, 2, MODES, 1, width), F32),
             pltpu.VMEM((2, 2) + tile, F32),
             pltpu.VMEM((2, 2, 2, 1, width), F32),
             pltpu.VMEM((2, 2, 2, 1, width), F32),

time: 15.5 us -> 15.4 us (level)
  no operation moved by 1% of the time
where the time goes in v5:
time: 15.4 us; the launch traced here: 15.2 us
  Pallas kernels  14.6 us (95%)
  between operations  0.64 us (4%)
    pallas_call x1, Pallas kernels, per_device(): pl.pallas_call(functools.partial(exchange, sizes), out_shape=(jax.ShapeDt...  13.1 us
    pallas_call x1, Pallas kernels, per_device(): pl.pallas_call(apply, out_shape=(jax.ShapeDtypeStruct((19, depth * rows,...  1.48 us

profile of v5, /device:TPU:0, one launch (start us, length us, event | category | flops | bytes accessed | tf_op | source)
XLA Modules:
  0.0 15.2 jit_solution(7192971044434047831)
XLA Ops:
  0.6 13.1 %shard_map.103 = (f32[19,144,128]{2,1,0:T(8,128)S(1)}, f32[12,18,8,128]{3,2,1,0:T(8,128)S(1)}, f32[2,12,24,128]{3,2,1,0:T(8,128)S(1)}, f32[2,2,8,128]{3,2,1,0:T(...) custom-call(f32[19,16,8,128]{3,2,1,0:T(8,128)} %pops_in.1, ...), custom_call_target="tpu_custom_call" | custom-call | tf_op jit(solution)/shard_map/pallas_call | solution.py:682
  13.7 1.5 %shard_map.104 = (f32[19,128,128]{2,1,0:T(8,128)}, f32[1,40]{1,0:T(1,128)}, f32[1,12]{1,0:T(1,128)}) custom-call(f32[19,144,128]{2,1,0:T(8,128)S(1)} %get-tuple-element.14.pre, f32[12,18,8,128]{3,2,1,0:T(8,128)S(1)} %get-tuple-element.15.flux_m, f32[2,12,24,128]{3,2,1,0:T(8,128)S(1)} %get-tuple-element.16.flux_x, ...), custom_call_target="tpu_custom_call" | custom-call | tf_op jit(solution)/shard_map/pallas_call | solution.py:750
